TPU v7x, 256 devices: a whole 4x4x8 slice. The times are simulated.
256 devices in a mesh: dp: 4 (over y), tm: 64 (over z, x, core).
Axes of the slice: x: 4, y: 4, z: 8, core: 2. Of those that a mesh axis runs over, the one named last changes fastest.
Arguments:
- video_tile: bfloat16 [4, 128, 16, 16, 256], P('dp', 'tm'), may hold values from -30 to 30
- clip_lengths: int32 [4, 6], P('dp'), may hold values from 1 to 48, 128 in all within a row
- kernels: bfloat16 [1, 3, 3, 3, 256, 256], replicated, may hold values from -0.078125 to 0.078125
- norm_gains: float32 [1, 256], replicated, may hold values from 0.5 to 2
- norm_shifts: float32 [1, 256], replicated, may hold values from -1 to 1
- cotangent: bfloat16 [4, 128, 16, 16, 256], P('dp', 'tm'), may hold values from -6 to 6
Outputs:
- outputs: bfloat16 [4, 128, 16, 16, 256], P('dp', 'tm')
- input_grads: bfloat16 [4, 128, 16, 16, 256], P('dp', 'tm')
- weight_grads: float32 [1, 27, 65536], P(None, None, ('dp', 'tm'))
Inputs may be any that keep to these rules, and one draw needn't show every extreme that they name: `clip_lengths`: each row lists 6 clip lengths in frames, in order, summing to 128; the longest is exactly 48.
All inputs are finite; a program needn't handle non-finite values.
Results may differ from a plain program's by a relative error of at most 0.0034.
Values may be sent and summed in bfloat16 or wider, within the bound.
A program may use at most 128 MiB of HBM per device.

v0:
```python
import math

import jax
import jax.numpy as jnp
from jax import lax
from jax.sharding import PartitionSpec as P

GROUPS = 32
BLOCKS = 1


EPS = 1e-05


def from_behind(shard, axis, by):
    devices = lax.axis_size(axis)
    pairs = [(i, i + by) for i in range(devices) if 0 <= i + by < devices]
    return lax.ppermute(shard, axis, pairs)


def entering(shard, axis, combine, identity, reverse):
    devices, position = (lax.axis_size(axis), lax.axis_index(axis))
    everything = jax.tree.map(lambda part: lax.all_gather(part, axis), shard)
    start = jax.tree.map(
        lambda part, zero: jnp.broadcast_to(jnp.asarray(zero, part.dtype), part.shape),
        shard,
        identity,
    )

    def turn(k, before):
        at = devices - 1 - k if reverse else k
        reached = at > position if reverse else at < position
        new = combine(before, jax.tree.map(lambda part: part[at], everything))
        return jax.tree.map(lambda a, b: jnp.where(reached, a, b), new, before)

    return lax.fori_loop(0, devices, turn, start)


def clip_of(moments, starts):
    return jnp.sum((starts[None, :] <= moments[:, None]).astype(jnp.int32), axis=1) - 1


def taps_forward(act_ext, kernel, keep_mask):
    frames = act_ext.shape[0] - 2
    height = act_ext.shape[1]
    tile_width = act_ext.shape[2]
    channels = act_ext.shape[3]
    padded = jnp.pad(act_ext, ((0, 0), (1, 1), (1, 1), (0, 0)))
    summed = jnp.zeros((frames * height * tile_width, channels), jnp.float32)
    for delay_step in range(3):
        factor = keep_mask[:, delay_step][:, None, None, None]
        for row_off in range(3):
            for col_off in range(3):
                sliced = (
                    padded[
                        2 - delay_step : 2 - delay_step + frames,
                        row_off : row_off + height,
                        col_off : col_off + tile_width,
                    ]
                    * factor
                )
                summed = summed + jnp.dot(
                    sliced.reshape(-1, channels),
                    kernel[delay_step, row_off, col_off],
                    preferred_element_type=jnp.float32,
                )
    return summed.reshape(frames, height, tile_width, channels)


def taps_backward(cot_ext, kernel, back_mask):
    frames = cot_ext.shape[0] - 2
    height = cot_ext.shape[1]
    tile_width = cot_ext.shape[2]
    channels = cot_ext.shape[3]
    padded = jnp.pad(cot_ext, ((0, 0), (1, 1), (1, 1), (0, 0)))
    summed = jnp.zeros((frames * height * tile_width, channels), jnp.float32)
    for delay_step in range(3):
        factor = back_mask[delay_step : delay_step + frames, delay_step][:, None, None, None]
        for row_off in range(3):
            for col_off in range(3):
                sliced = (
                    padded[
                        delay_step : delay_step + frames,
                        2 - row_off : 2 - row_off + height,
                        2 - col_off : 2 - col_off + tile_width,
                    ]
                    * factor
                )
                summed = summed + jnp.dot(
                    sliced.reshape(-1, channels),
                    kernel[delay_step, row_off, col_off].T,
                    preferred_element_type=jnp.float32,
                )
    return summed.reshape(frames, height, tile_width, channels)


def lag_weights(act_ext, upstream, keep_mask, delay_step):
    frames = act_ext.shape[0] - 2
    height = act_ext.shape[1]
    tile_width = act_ext.shape[2]
    channels = act_ext.shape[3]
    padded = jnp.pad(act_ext, ((0, 0), (1, 1), (1, 1), (0, 0)))
    flat_up = upstream.reshape(-1, channels)
    factor = keep_mask[:, delay_step][:, None, None, None]
    pieces = []
    for row_off in range(3):
        for col_off in range(3):
            sliced = (
                padded[
                    2 - delay_step : 2 - delay_step + frames,
                    row_off : row_off + height,
                    col_off : col_off + tile_width,
                ]
                * factor
            )
            pieces.append(
                lax.dot_general(
                    sliced.reshape(-1, channels),
                    flat_up,
                    (((0,), (0,)), ((), ())),
                    preferred_element_type=jnp.float32,
                )
            )
    return jnp.stack(pieces)


def grouped_view(values, groups):
    return values.astype(jnp.float32).reshape(
        values.shape[0], values.shape[1], values.shape[2], groups, -1
    )


def frame_sums(inputs, groups):
    grouped = grouped_view(inputs, groups)
    return (jnp.sum(grouped, axis=(1, 2, 4)), jnp.sum(grouped * grouped, axis=(1, 2, 4)))


def spread_groups(stat):
    return stat[:, None, None, :, None]


def normalize(inputs, first_cum, second_cum, counted, gain, offset, groups):
    per_frame = inputs.shape[1] * inputs.shape[2] * (inputs.shape[3] // groups)
    entries = counted[:, None] * per_frame
    group_mean = first_cum / entries
    variance = second_cum / entries - group_mean * group_mean
    inv_std = lax.rsqrt(variance + EPS)
    grouped = grouped_view(inputs, groups)
    unit = (grouped - spread_groups(group_mean)) * spread_groups(inv_std)
    normed = unit.reshape(inputs.shape) * gain + offset
    return (normed, jax.nn.silu(normed).astype(jnp.bfloat16), group_mean, inv_std, entries)


def norm_backward(inputs, normed, act_grad, group_mean, inv_std, entries, gain, groups):
    sigmoid = jax.nn.sigmoid(normed)
    slope = act_grad * sigmoid * (1.0 + normed * (1.0 - sigmoid))
    grouped_grad = (slope * gain).reshape(
        inputs.shape[0], inputs.shape[1], inputs.shape[2], groups, -1
    )
    centred = grouped_view(inputs, groups) - spread_groups(group_mean)
    radius_grad = jnp.sum(grouped_grad * centred, axis=(1, 2, 4))
    mean_grad = -jnp.sum(grouped_grad, axis=(1, 2, 4)) * inv_std
    cubed = inv_std * inv_std * inv_std
    first_grad = (mean_grad + radius_grad * cubed * group_mean) / entries
    second_grad = -0.5 * radius_grad * cubed / entries
    direct = grouped_grad * spread_groups(inv_std)
    return (direct, first_grad, second_grad)


def finish(upstream, inputs, direct, first_back, second_back, groups):
    grouped = grouped_view(inputs, groups)
    summed = (
        grouped_view(upstream, groups)
        + direct
        + spread_groups(first_back)
        + 2.0 * grouped * spread_groups(second_back)
    )
    return summed.reshape(inputs.shape).astype(jnp.bfloat16)


def neighbour(frames_part, offset):
    return from_behind(frames_part, "tm", offset)


def join_stats(earlier, later):
    flag_early, early_first, early_second = earlier
    flag_late, late_first, late_second = later
    passing = 1.0 - flag_late
    return (
        jnp.maximum(flag_early, flag_late),
        late_first + passing * early_first,
        late_second + passing * early_second,
    )


def chain(element, backwards):
    groups = element[1].shape[0]
    identity = (
        jnp.zeros((), jnp.float32),
        jnp.zeros((groups,), jnp.float32),
        jnp.zeros((groups,), jnp.float32),
    )
    return entering(element, "tm", join_stats, identity, backwards)


def reduce_terms(terms):
    return lax.psum_scatter(terms, ("dp", "tm"), scatter_dimension=1, tiled=True)


def local(video_tile, clip_lengths, kernels, norm_gains, norm_shifts, cotangent):
    inputs = video_tile[0]
    frames = inputs.shape[0]
    channels = inputs.shape[3]
    lengths = clip_lengths[0]
    starts = jnp.cumsum(lengths) - lengths
    first_frame = lax.axis_index("tm") * frames
    beside_all = first_frame - 2 + jnp.arange(frames + 4, dtype=jnp.int32)
    clips_around = clip_of(beside_all, starts)
    clips = clips_around[2 : 2 + frames]
    before = clips_around[1]
    after = clips_around[2 + frames]
    moments = beside_all[2 : 2 + frames]
    local_order = jnp.arange(frames, dtype=jnp.int32)
    within = (
        (clips[:, None] == clips[None, :]) & (local_order[None, :] <= local_order[:, None])
    ).astype(jnp.float32)
    clip_begin = jnp.max(jnp.where(starts[None, :] <= moments[:, None], starts[None, :], 0), axis=1)
    counted = (moments - clip_begin + 1).astype(jnp.float32)
    keep_mask = jnp.stack(
        [
            clips == clips_around[2 - delay_step : 2 - delay_step + frames]
            for delay_step in range(3)
        ],
        axis=1,
    ).astype(jnp.bfloat16)
    back_mask = jnp.stack(
        [
            clips_around[2 : frames + 4] == clips_around[2 - delay_step : frames + 4 - delay_step]
            for delay_step in range(3)
        ],
        axis=1,
    ).astype(jnp.bfloat16)
    continues = (clips == before).astype(jnp.float32)
    resumes = (clips == after).astype(jnp.float32)
    flag_forward = (clips[frames - 1] != before).astype(jnp.float32)
    flag_backward = (clips[0] != after).astype(jnp.float32)
    current = inputs
    layer_index = 0
    first_sums, second_sums = frame_sums(current, GROUPS)
    local_first = jnp.dot(within, first_sums, precision=lax.Precision.HIGHEST)
    local_second = jnp.dot(within, second_sums, precision=lax.Precision.HIGHEST)
    _, carried_first, carried_second = chain(
        (flag_forward, local_first[frames - 1], local_second[frames - 1]), False
    )
    first_cum = local_first + continues[:, None] * carried_first[None, :]
    second_cum = local_second + continues[:, None] * carried_second[None, :]
    normed, activation, group_mean, inv_std, entries = normalize(
        current,
        first_cum,
        second_cum,
        counted,
        norm_gains[layer_index],
        norm_shifts[layer_index],
        GROUPS,
    )
    previous = neighbour(activation, 1)
    act_ext = jnp.concatenate([previous, activation], axis=0)
    conv_out = taps_forward(act_ext, kernels[layer_index], keep_mask)
    stored = [(current, normed, group_mean, inv_std, entries, act_ext)]
    current = (current.astype(jnp.float32) + conv_out).astype(jnp.bfloat16)
    scale_factor = 1.0 / math.sqrt(
        lax.axis_size("dp") * lax.axis_size("tm") * frames * inputs.shape[1] * inputs.shape[2]
    )
    upstream = cotangent[0]
    weight_blocks = [None] * BLOCKS
    for layer_index in reversed(range(BLOCKS)):
        held, normed, group_mean, inv_std, entries, act_ext = stored[layer_index]
        following = neighbour(upstream, -1)
        cot_ext = jnp.concatenate([upstream, following], axis=0)
        act_grad = taps_backward(cot_ext, kernels[layer_index], back_mask)
        lag_parts = [
            lag_weights(act_ext, upstream, keep_mask, delay_step) for delay_step in range(3)
        ]
        terms = (jnp.concatenate(lag_parts, axis=0) * scale_factor).reshape(27, channels * channels)
        weight_blocks[layer_index] = reduce_terms(terms)
        direct, first_grad, second_grad = norm_backward(
            held, normed, act_grad, group_mean, inv_std, entries, norm_gains[layer_index], GROUPS
        )
        local_first = jnp.dot(within.T, first_grad, precision=lax.Precision.HIGHEST)
        local_second = jnp.dot(within.T, second_grad, precision=lax.Precision.HIGHEST)
        _, carried_first, carried_second = chain(
            (flag_backward, local_first[0], local_second[0]), True
        )
        first_back = local_first + resumes[:, None] * carried_first[None, :]
        second_back = local_second + resumes[:, None] * carried_second[None, :]
        upstream = finish(upstream, held, direct, first_back, second_back, GROUPS)
    weight_grads = jnp.stack(weight_blocks)
    return (current[None], upstream[None], weight_grads)


def solution(mesh):
    placed = (
        P("dp", "tm", None, None, None),
        P("dp", None),
        P(),
        P(),
        P(),
        P("dp", "tm", None, None, None),
    )
    return jax.shard_map(
        local,
        mesh=mesh,
        in_specs=placed,
        out_specs=(
            P("dp", "tm", None, None, None),
            P("dp", "tm", None, None, None),
            P(None, None, ("dp", "tm")),
        ),
        check_vma=False,
    )
```

profile of v0, /device:TPU:32, one launch (start us, length us, event | category | flops | bytes accessed | tf_op | source)
XLA Modules:
  0.0 1745.7 jit_solution(2052748904988837918)
XLA Ops:
  7.2 3.7 collective-permute-start.1
  13.5 1.0 fusion.2
  15.1 40.3 %all-gather = f32[64,1,32]{2,1,0:T(1,128)S(1)} all-gather(f32[1,1,32]{2,1,0:T(1,128)S(1)} %slice_bitcast_fusion.90), channel_id=1, replica_groups=mesh['dp'=4,'tm'=64] {'tm'}, dimensions={0}, use_global_device_ids=true | all-gather | bytes 8320 | tf_op jit(solution)/shard_map/all_gather | solution.py:23
  56.7 1.4 compare_convert_fusion
  59.4 38.2 %all-gather.1 = f32[64,1,32]{2,1,0:T(1,128)S(1)} all-gather(f32[1,1,32]{2,1,0:T(1,128)S(1)} %slice_bitcast_fusion.89), channel_id=1, replica_groups=mesh['dp'=4,'tm'=64] {'tm'}, dimensions={0}, use_global_device_ids=true | all-gather | bytes 8320 | tf_op jit(solution)/shard_map/all_gather | solution.py:23
  97.6 1.3 dynamic-slice
  100.3 108.2 %all-reduce.4 = (f32[64]{0:T(128)S(1)}, f32[64]{0:T(128)S(1)}) all-reduce(f32[64]{0:T(128)S(1)} %dynamic-update-slice, f32[64]{0:T(128)S(1)} %dynamic-update-slice.1), channel_id=1, replica_groups=mesh['dp'=4,'tm'=64] {'tm'}, use_global_device_ids=true, to_apply=%add.2 | all-reduce | flops 128 | bytes 1024
  208.5 82.2 %while.34 = (s32[]{:T(128)}, f32[32]{0:T(128)S(1)}, f32[32]{0:T(128)S(1)}, s32[]{:T(128)}, f32[64,32]{1,0:T(8,128)S(1)}, /*index=5*/f32[64]{0:T(128)S(1)}, f32[6...) while((s32[]{:T(128)}, f32[32]{0:T(128)S(1)}, f32[32]{0:T(128)S(1)}, s32[]{:T(128)}, ...), condition=%wide.region_7.8_spmd.clone, body=%wide.region_6.7_spmd.clone.sunk | while | flops 261 | bytes 929 | solution.py:36
  291.6 1.2 broadcast_multiply_fusion.4
  292.8 1.9 collective-permute-start
  294.9 1.2 convolution_bitcast_fusion.22
  296.2 4.5 copy.30
  302.9 1.0 copy.35
  313.1 2.9 reshape.517
  316.0 5.4 fusion.93
  321.9 54.3 %all-gather.2 = f32[64,1,32]{2,1,0:T(1,128)S(1)} all-gather(f32[1,1,32]{2,1,0:T(1,128)S(1)} %slice_bitcast_fusion.82), channel_id=1, replica_groups=mesh['dp'=4,'tm'=64] {'tm'}, dimensions={0}, use_global_device_ids=true | all-gather | bytes 8320 | tf_op jit(solution)/shard_map/all_gather | solution.py:23
  376.2 38.1 %all-gather.3 = f32[64,1,32]{2,1,0:T(1,128)S(1)} all-gather(f32[1,1,32]{2,1,0:T(1,128)S(1)} %slice_bitcast_fusion.81), channel_id=1, replica_groups=mesh['dp'=4,'tm'=64] {'tm'}, dimensions={0}, use_global_device_ids=true | all-gather | bytes 8320 | tf_op jit(solution)/shard_map/all_gather | solution.py:23
  416.2 1.0 copy.31
  417.4 1.0 copy.32
  422.5 1.0 copy.37
  423.8 1.0 copy.38
  425.0 1.0 copy.39
  427.0 1.2 copy.40
  428.4 1.0 copy.41
  429.7 1.0 copy.42
  430.9 1.0 copy.43
  432.2 1.0 copy.44
  433.6 1.0 copy.45
  434.8 1.0 copy.46
  436.1 1.0 copy.47
  437.3 1.0 copy.48
  439.8 1.0 copy.50
  441.1 1.0 copy.51
  442.3 1.0 copy.52
  443.6 1.2 copy.53
  445.1 1.0 copy.54
  447.5 1.0 copy.56
  448.8 1.0 copy.57
  449.8 25.2 %concatenate.93 = f32[27,65536]{1,0:T(8,128)} concatenate(f32[1,65536]{1,0:T(1,128)} %bitcast.631, f32[1,65536]{1,0:T(1,128)} %bitcast.632, f32[1,65536]{1,0:T(1,128)} %bitcast.633, f32[1,65536]{1,0:T(1,128)} %bitcast.634, f32[1,65536]{1,0:T(1,128)} %bitcast.630, f32[1,65536]{1,0:T(1,128)} %bitcast.635, f32[1,65536]{1,0:T(1,128)} %bitcast.636, f32[1,65536]{1,0:T(1,128)} %bitcast.637, ...), dimensions={0} | concatenate | bytes 14155776 | tf_op jit(solution)/shard_map/concatenate | solution.py:284
  474.9 7.4 broadcast_multiply_fusion
  482.3 81.8 %while.35 = (s32[]{:T(128)}, f32[32]{0:T(128)S(1)}, f32[32]{0:T(128)S(1)}, s32[]{:T(128)}, f32[64,32]{1,0:T(8,128)S(1)}, /*index=5*/f32[64]{0:T(128)S(1)}, f32[6...) while((s32[]{:T(128)}, f32[32]{0:T(128)S(1)}, ...), condition=%wide.region_12.13_spmd.clone, body=%wide.region_11.12_spmd.clone.sunk | while | flops 265 | bytes 991 | solution.py:36
  564.5 1.3 fusion.85
  565.8 1.2 fusion.83
  567.0 1.3 convolution_add_fusion.49
  568.3 1.2 convolution_add_fusion.48
  575.2 1.2 fusion.19
  576.3 1161.1 %reduce-scatter.2.cloned.1.call-done = f32[27,256]{1,0:T(8,128)} async-done(((f32[27,65536]{1,0:T(8,128)}), f32[27,256]{1,0:T(8,128)}) %reduce-scatter.2.cloned.1.call-update) | async-done | bytes 27664 | tf_op jit(solution)/shard_map/reduce_scatter | solution.py:207
  1737.4 1.4 stack.26
  (489 shorter events, 116.7 us)
Async XLA Ops:
  7.2 1730.3 %reduce-scatter.2.cloned.1.call-start = ((), (), s32[]{:S(2)}) async-start(), calls=%async_computation.1 | async-start | bytes 8421376 | tf_op jit(solution)/shard_map/reduce_scatter | solution.py:207
  7.2 296.8 %collective-permute-start.1 = (bf16[2,16,16,256]{3,2,1,0:T(8,128)(2,1)}, bf16[2,16,16,256]{3,2,1,0:T(8,128)(2,1)S(1)}, u32[]{:S(2)}, u32[]{:S(2)}) collective-permute-start(bf16[2,16,16,256]{3,2,1,0:T(8,128)(2,1)} %bitcast.489), channel_id=1, source_target_pairs={{1,0},{2,1},{3,2},{4,3},{5,4},{6,5},{7,6},{8,7},{9,8},{10,9},{11,1... | collective-permute-start | bytes 786440 | tf_op jit(solution)/shard_map/ppermute | solution.py:18
  12.4 288.9 %copy-start.40 = (f32[1,256]{1,0:T(1,128)S(1)}, f32[1,256]{1,0:T(1,128)}, u32[]{:S(2)}) copy-start(f32[1,256]{1,0:T(1,128)} %param.14) | copy-start | bytes 3076
  12.6 289.4 %copy-start.41 = (f32[1,256]{1,0:T(1,128)S(1)}, f32[1,256]{1,0:T(1,128)}, u32[]{:S(2)}) copy-start(f32[1,256]{1,0:T(1,128)} %param.13) | copy-start | bytes 3076
  208.5 95.4 %copy-start = (bf16[1,2,16,16,256]{4,3,2,1,0:T(8,128)(2,1)S(1)}, bf16[1,2,16,16,256]{4,3,2,1,0:T(8,128)(2,1)}, u32[]{:S(2)}) copy-start(bf16[1,2,16,16,256]{4,3,2,1,0:T(8,128)(2,1)} %param.15) | copy-start | bytes 786436
  292.8 2.2 copy-start.14
  292.8 121.5 %copy-start.36 = (bf16[2,16,16,256]{3,2,1,0:T(8,128)(2,1)}, bf16[2,16,16,256]{3,2,1,0:T(8,128)(2,1)S(1)}, u32[]{:S(2)}) copy-start(bf16[2,16,16,256]{3,2,1,0:T(8,128)(2,1)S(1)} %get-tuple-element.392) | copy-start | bytes 786436
  292.8 121.5 %collective-permute-start = (bf16[2,16,16,256]{3,2,1,0:T(8,128)(2,1)S(1)}, bf16[2,16,16,256]{3,2,1,0:T(8,128)(2,1)S(1)}, u32[]{:S(2)}, u32[]{:S(2)}) collective-permute-start(bf16[2,16,16,256]{3,2,1,0:T(8,128)(2,1)S(1)} %get-tuple-element.392), channel_id=1, source_target_pairs={{0,1},{1,2},{2,3},{3,4},{4,5},{5,6},{6,7},{7,8},{8,9},{9,10},{10,1... | collective-permute-start | bytes 786440 | tf_op jit(solution)/shard_map/ppermute | solution.py:18
  302.9 2.1 copy-start.1
  414.3 0.7 copy-start.38
  415.9 6.6 copy-start.6
  415.9 6.6 copy-start.8
  415.9 6.6 copy-start.10
  415.9 6.6 copy-start.12
  415.9 6.6 copy-start.13
  415.9 7.6 copy-start.4
  418.7 7.3 copy-start.37
  418.7 7.3 copy-start.39
  426.6 6.9 copy-start.24
  426.6 6.9 copy-start.26
  426.6 6.9 copy-start.28
  426.6 6.9 copy-start.30
  426.6 6.9 copy-start.32
  426.6 6.9 copy-start.34
  426.7 7.9 copy-start.22
  426.7 9.1 copy-start.20
  426.7 10.4 copy-start.18
  426.7 16.6 copy-start.16
  564.5 5.0 copy-start.2
  564.5 5.0 copy-start.11
  564.5 5.3 copy-start.15
  565.8 4.2 copy-start.9
  567.0 3.3 copy-start.7
  568.3 2.3 copy-start.5
  569.8 1.2 copy-start.35
  570.0 1.2 copy-start.33
  570.3 1.2 copy-start.31
  570.5 1.2 copy-start.29
  570.8 1.3 copy-start.27
  571.0 1.2 copy-start.25
  571.3 1.2 copy-start.23
  571.5 1.2 copy-start.21
  571.8 1.2 copy-start.19
  573.0 1.2 copy-start.17
  574.0 1.2 copy-start.3
Sparse Core Ops, SparseCore 0:
  482.4 1254.9 reduce-scatter.1
where the time goes:
time: 1770 us; the launch traced here: 1750 us
  waiting for transfers between devices  1160 us (66%)
  blocking collectives  279 us (16%)
  local copies, waits for them, and re-layouts  144 us (8%)
  loops' own time  84.4 us (5%)
  other arithmetic  27.2 us (2%)
  matrix products  26 us (1%)
  between operations  17.9 us (1%)
    reduce_scatter x1, waiting for transfers between devices, reduce_terms(): lax.psum_scatter(terms, ('dp', 'tm'), scatter_dimension=1, tiled=True)  1160 us
    all_gather x4, blocking collectives, entering(): everything = jax.tree.map(lambda part: lax.all_gather(part, axis), shard)  171 us
    unnamed x1, blocking collectives  108 us
    another operation x2, loops' own time, entering(): return lax.fori_loop(0, devices, turn, start)  84.4 us
    dynamic_slice x128, local copies, waits for them, and re-layouts, turn(): new = combine(before, jax.tree.map(lambda part: part[at], everything))  76.9 us
  transfers between devices with their start and end apart: 3, of which 1 were waited for; matrix products, arithmetic and copies ran while one was open for 7% of the time, Pallas kernels for 0%

commit v1 on v0

v1 whole, which is shorter than its diff:
```python
import functools
import math

import jax
import jax.numpy as jnp
from jax import lax
from jax.experimental import pallas as pl
from jax.experimental.pallas import tpu as pltpu
from jax.sharding import PartitionSpec as P

EPS = 1e-05
NX = 4
NC = 2
GROUP = NX * NC
TAPS = 27
X_SLOTS = ((0, 5), (5, 4), (9, 5))
Y_SLOTS = ((0, 4), (4, 5), (9, 4))
MESH = pl.DeviceIdType.MESH
F32 = jnp.float32
BF16 = jnp.bfloat16


def iota(shape, dim):
    return lax.broadcasted_iota(jnp.int32, shape, dim)


def clip_begin(starts, t):
    begin = jnp.int32(0)
    for start in starts:
        begin = jnp.where(start <= t, start, begin)
    return begin


def clip_end(starts, t, frames):
    end = jnp.int32(frames)
    for start in reversed(starts):
        end = jnp.where(start > t, start, end)
    return end


def flag(condition):
    return jnp.where(condition, jnp.float32(1.0), jnp.float32(0.0))


def dot(a, b, contract=(1, 0), precision=None):
    return lax.dot_general(
        a,
        b,
        (((contract[0],), (contract[1],)), ((), ())),
        preferred_element_type=F32,
        precision=precision,
    )


def sigmoid(z):
    return 0.5 * jnp.tanh(0.5 * z) + 0.5


def pack_rows(rows):
    place = iota((8, 256), 0)
    stacked = jnp.zeros((8, 256), F32)
    for k, row in enumerate(rows):
        stacked = jnp.where(place == k, row, stacked)
    gather = ((iota((256, 128), 0) >> 3) == (iota((256, 128), 1) & 31)).astype(F32)
    grouped = dot(stacked, gather, precision=lax.Precision.HIGHEST)
    mine = (iota((8, 128), 1) >> 5) == iota((8, 128), 0)
    return jnp.sum(jnp.where(mine, grouped, 0.0), axis=0, keepdims=True)


def spread(rows):
    lanes = iota((8, 128), 1)
    clean = jnp.where(lanes < 32, rows, 0.0)
    matrix = (iota((128, 256), 0) == (iota((128, 256), 1) >> 3)).astype(F32)
    return dot(clean, matrix, precision=lax.Precision.HIGHEST)


def masked_rows(buffer, bounds):
    values = buffer[...]
    frame = 2 * iota(values.shape, 0) + (iota(values.shape, 2) >> 6)
    place = iota((8, 128), 0)
    rows = jnp.zeros((8, 128), F32)
    for k, (low, high) in enumerate(bounds):
        inside = (frame >= low) & (frame < high)
        total = jnp.sum(jnp.where(inside, values, 0.0), axis=0)
        rows = jnp.where(place == k, total, rows)
    return rows + pltpu.roll(rows, 64, 1)


def kernel(
    nz,
    ny,
    scale,
    lens,
    gain,
    shift,
    video,
    cot,
    kern,
    out,
    grads,
    wgrads,
    xw,
    gwin,
    kv,
    gim,
    aim,
    act,
    lhs,
    stat,
    dstat,
    mean_rows,
    scale_rows,
    inv_rows,
    da,
    sx1,
    rx1,
    sy1,
    ry1,
    sx2,
    rx2,
    sy2,
    ry2,
    total3,
    s3,
    r3,
    out_v,
    grads_v,
    load_sem,
    halo_send,
    halo_recv,
    chain_send,
    chain_recv,
    one_send,
    one_recv,
    two_send,
    two_recv,
    three_send,
    three_recv,
    store_sem,
):
    y = lax.axis_index("dp")
    tm = lax.axis_index("tm")
    core = lax.rem(tm, NC)
    x = lax.rem(tm // NC, NX)
    z = tm // GROUP
    within = lax.rem(tm, GROUP)
    chip = tm // NC
    chips = nz * NX
    frames = 2 * nz * GROUP
    base = 4 * chip
    own = 2 * tm

    def at(tm_index, dp_index=None):
        return {"dp": y if dp_index is None else dp_index, "tm": tm_index}

    def x_peer(d):
        return z * GROUP + lax.rem(x + d, NX) * NC + core

    def z_peer(d):
        return lax.rem(z + d, nz) * GROUP + within

    def y_peer(d):
        return lax.rem(y + d, ny)

    def group_peer(d):
        return z * GROUP + lax.rem(within + d, GROUP)

    next_chip = lax.rem(chip + 1, chips)
    prev_chip = lax.rem(chip + chips - 1, chips)

    load_x = pltpu.make_async_copy(video.at[0], xw.at[pl.ds(2 + 2 * core, 2)], load_sem.at[0])
    load_g = pltpu.make_async_copy(cot.at[0], gwin.at[pl.ds(2 * core, 2)], load_sem.at[1])
    load_k = [
        pltpu.make_async_copy(kern.at[0, lag], kv.at[lag], load_sem.at[2 + lag]) for lag in range(3)
    ]
    load_x.start()
    load_g.start()

    barrier = pltpu.get_barrier_semaphore()

    def greet(device):
        pl.semaphore_signal(barrier, inc=1, device_id=device, device_id_type=MESH)

    def greet_group(d, carry):
        greet(at(group_peer(d)))
        return carry

    def greet_z(d, carry):
        greet(at(z_peer(d)))
        return carry

    def greet_y(d, carry):
        greet(at(tm, y_peer(d)))
        return carry

    lax.fori_loop(1, GROUP, greet_group, 0)
    lax.fori_loop(1, nz, greet_z, 0)
    lax.fori_loop(1, ny, greet_y, 0)
    for c in range(NC):
        greet(at(next_chip * NC + c))
        greet(at(prev_chip * NC + c))
    for copy in load_k:
        copy.start()

    starts = []
    begin = jnp.int32(0)
    for k in range(6):
        starts.append(begin)
        begin = begin + lens[0, k]

    load_x.wait()
    sums = []
    for f in range(2):
        values = xw[2 + 2 * core + f].reshape(256, 256).astype(F32)
        sums.append(jnp.sum(values, axis=0, keepdims=True))
        sums.append(jnp.sum(values * values, axis=0, keepdims=True))
    stat[pl.ds(tm, 1)] = pack_rows(sums).reshape(1, 1, 128)

    pl.semaphore_wait(barrier, (GROUP - 1) + (nz - 1) + (ny - 1) + 2 * NC)

    def first_copy(buffer, kind, d):
        mine = buffer.at[pl.ds(tm, 1)]
        return pltpu.make_async_remote_copy(
            src_ref=mine,
            dst_ref=mine,
            send_sem=chain_send.at[kind, d],
            recv_sem=chain_recv.at[kind, d],
            device_id=at(group_peer(d)),
            device_id_type=MESH,
        )

    def second_copy(buffer, kind, d):
        mine = buffer.at[pl.ds(z * GROUP, GROUP)]
        return pltpu.make_async_remote_copy(
            src_ref=mine,
            dst_ref=mine,
            send_sem=chain_send.at[kind, d],
            recv_sem=chain_recv.at[kind, d],
            device_id=at(z_peer(d)),
            device_id_type=MESH,
        )

    def loop(count, act_on):
        def body(d, carry):
            act_on(d)
            return carry

        lax.fori_loop(1, count, body, 0)

    loop(GROUP, lambda d: first_copy(stat, 0, d).start())

    def halo(src, dst, sent, received, device):
        return pltpu.make_async_remote_copy(
            src_ref=src,
            dst_ref=dst,
            send_sem=halo_send.at[sent],
            recv_sem=halo_recv.at[received],
            device_id=at(device),
            device_id_type=MESH,
        )

    partner = chip * NC + 1 - core
    own_g = gwin.at[pl.ds(2 * core, 2)]
    own_x = xw.at[pl.ds(2 + 2 * core, 2)]
    after_g = gwin.at[pl.ds(4, 2)]
    g_partner = halo(cot.at[0], own_g, 0, 0, partner)
    x_partner = halo(video.at[0], own_x, 1, 1, partner)
    g_back = [halo(cot.at[0], after_g, 2 + c, 2, prev_chip * NC + c) for c in range(NC)]
    x_ahead = halo(video.at[0], xw.at[pl.ds(0, 2)], 4, 3, next_chip * NC)
    g_partner.start()

    @pl.when(core == 0)
    def _():
        g_back[1].start()
        g_back[0].start()

    x_partner.start()

    @pl.when(core == 1)
    def _():
        x_ahead.start()

    pixel, source = iota((256, 256), 0), iota((256, 256), 1)
    right = ((source == pixel + 1) & ((pixel & 15) != 15)).astype(BF16)
    left = ((source == pixel - 1) & ((pixel & 15) != 0)).astype(BF16)
    both = jnp.concatenate([right, left], axis=0)

    def widen(target, k, values, first, last):
        shifted = dot(both, values).astype(BF16)
        target[k, 1:17, :, 256 * first : 256 * first + 256] = shifted[:256].reshape(16, 16, 256)
        target[k, 1:17, :, 256:512] = values.reshape(16, 16, 256)
        target[k, 1:17, :, 256 * last : 256 * last + 256] = shifted[256:].reshape(16, 16, 256)
        target[k, 0:1] = jnp.zeros((1, 16, 768), BF16)
        target[k, 17:18] = jnp.zeros((1, 16, 768), BF16)

    def widen_g(v, carry):
        widen(gim, v, gwin[v].reshape(256, 256), 0, 2)
        return carry

    load_g.wait()
    g_partner.wait_recv()
    lax.fori_loop(0, 4, widen_g, 0)

    loop(GROUP, lambda d: first_copy(stat, 0, d).wait_recv())
    loop(nz, lambda d: second_copy(stat, 1, d).start())

    g_back[1].wait_recv()
    lax.fori_loop(4, 6, widen_g, 0)
    for copy in load_k:
        copy.wait()

    for lag in range(3):
        taken = jnp.concatenate(
            [
                gim[pl.ds(2 * core + lag, 2), 2 - i : 18 - i].reshape(512, 768)
                for i in range(3)
            ],
            axis=1,
        )
        weights = jnp.concatenate(
            [kv[lag, i, j] for i in range(3) for j in range(3)], axis=1
        )
        part = dot(taken, weights, (1, 1))
        for f in range(2):
            piece = part[256 * f : 256 * f + 256]
            if lag == 0:
                da[f] = piece
            else:
                keep = flag(own + f + lag < clip_end(starts, own + f, frames))
                da[f] = da[f] + keep * piece

    loop(nz, lambda d: second_copy(stat, 1, d).wait_recv())
    bounds, counted = [], jnp.zeros((8, 128), F32)
    for k in range(6):
        t = base - 2 + k
        b = clip_begin(starts, t)
        bounds.append((b, t + 1))
        count = jnp.maximum(t + 1 - b, 1).astype(F32)
        counted = jnp.where(iota((8, 128), 0) == k, count, counted)
    counted = jnp.maximum(counted, 1.0) * 2048.0
    averaged = masked_rows(stat, bounds) / counted
    squares = pltpu.roll(averaged, 96, 1)
    inv_std = lax.rsqrt(squares - averaged * averaged + EPS)
    mean_rows[...] = spread(averaged)
    wide_inv = spread(inv_std)
    inv_rows[...] = wide_inv
    scale_rows[...] = wide_inv * gain[...]

    def activate(k, carry):
        values = xw[k].reshape(256, 256).astype(F32)
        normed = (values - mean_rows[pl.ds(k, 1)]) * scale_rows[pl.ds(k, 1)] + shift[...]
        act[k] = (normed * sigmoid(normed)).astype(BF16)
        return carry

    x_partner.wait_recv()
    lax.fori_loop(2, 6, activate, 0)

    row, channel = iota((128, 256), 0), iota((128, 256), 1)
    wanted = 64 * ((row >> 3) & 3) + 8 * (row & 7) + 2 * (row >> 5) + core
    select = (channel == wanted).astype(BF16)
    blank = jnp.zeros((128, 256), BF16)
    for lag, v in ((0, 4), (0, 5), (1, 0), (1, 5), (2, 0), (2, 1)):
        lhs[128 * lag : 128 * lag + 128, 256 * v : 256 * v + 256] = blank
    for u in range(4):
        turned = dot(select, act[2 + u], (1, 1))
        end = clip_end(starts, base + u, frames)
        for lag in range(3):
            masked = turned if lag == 0 else turned * flag(base + u + lag < end)
            v = u + lag
            lhs[128 * lag : 128 * lag + 128, 256 * v : 256 * v + 256] = masked.astype(BF16)

    def one_x(i, d):
        low, count = X_SLOTS[i]
        target = lax.rem(x + d, NX)
        return pltpu.make_async_remote_copy(
            src_ref=sx1.at[target, pl.ds(low, count)],
            dst_ref=rx1.at[d, pl.ds(low, count)],
            send_sem=one_send.at[0, i, d],
            recv_sem=one_recv.at[0, i, d],
            device_id=at(x_peer(d)),
            device_id_type=MESH,
        )

    def one_y(i, d):
        low, count = Y_SLOTS[i]
        target = lax.rem(y + d, ny)
        return pltpu.make_async_remote_copy(
            src_ref=sy1.at[target, pl.ds(low, count)],
            dst_ref=ry1.at[d, pl.ds(low, count)],
            send_sem=one_send.at[1, i, d],
            recv_sem=one_recv.at[1, i, d],
            device_id=at(tm, y_peer(d)),
            device_id_type=MESH,
        )

    for i in range(3):
        terms = dot(lhs[...], gim[:, 2 - i : 18 - i].reshape(1536, 768))
        for lag in range(3):
            for j in range(3):
                n = 9 * i + 3 * lag + j
                block = terms[128 * lag : 128 * lag + 128, 256 * j : 256 * j + 256]
                for p in range(4):
                    if n % 2 == 0:
                        sx1[p, n // 2] = block[32 * p : 32 * p + 32].astype(BF16)
                    else:
                        rows = [block[32 * q + 8 * p : 32 * q + 8 * p + 8] for q in range(4)]
                        sy1[p, n // 2] = jnp.concatenate(rows, axis=0).astype(BF16)
        for d in (2, 1, 3):
            one_x(i, d).start()
            one_y(i, d).start()

    @pl.when(core == 0)
    def _():
        x_ahead.wait_recv()
        lax.fori_loop(0, 2, activate, 0)

    def widen_a(k, carry):
        widen(aim, k, act[2 * core + k], 2, 0)
        return carry

    lax.fori_loop(0, 4, widen_a, 0)
    for lag in range(3):
        taken = jnp.concatenate(
            [aim[2 - lag : 4 - lag, i : i + 16].reshape(512, 768) for i in range(3)], axis=1
        )
        part = dot(taken, kv[lag].reshape(2304, 256))
        for f in range(2):
            piece = part[256 * f : 256 * f + 256]
            if lag == 0:
                total = xw[2 + 2 * core + f].reshape(256, 256).astype(F32) + piece
            else:
                keep = flag(own + f - lag >= clip_begin(starts, own + f))
                total = total_f[f] + keep * piece
            if f == 0:
                first = total
            else:
                total_f = [first, total]
    for f in range(2):
        out_v[f] = total_f[f].reshape(16, 16, 256).astype(BF16)
    store_out = pltpu.make_async_copy(out_v, out.at[0], store_sem.at[0])
    store_out.start()

    lanes = iota((1, 128), 1)
    sums = []
    for f in range(2):
        k = 2 + 2 * core + f
        centred = xw[k].reshape(256, 256).astype(F32) - mean_rows[pl.ds(k, 1)]
        normed = centred * scale_rows[pl.ds(k, 1)] + shift[...]
        sig = sigmoid(normed)
        du = da[f] * (sig * (1.0 + normed * (1.0 - sig))) * gain[...]
        da[f] = du
        sums.append(jnp.sum(du, axis=0, keepdims=True))
        sums.append(jnp.sum(du * centred, axis=0, keepdims=True))
    packed = pack_rows(sums)
    row_of = iota((8, 128), 0)

    def pick(rows, k):
        return jnp.sum(jnp.where(row_of == k, rows, 0.0), axis=0, keepdims=True)

    answer = jnp.zeros((1, 128), F32)
    for f in range(2):
        k = 2 + 2 * core + f
        mean_k, inv_k, n_k = pick(averaged, k), pick(inv_std, k), pick(counted, k)
        sum_du = pltpu.roll(packed, 64, 1) if f else packed
        dr = pltpu.roll(sum_du, 96, 1)
        cubed = inv_k * inv_k * inv_k
        dc1 = (dr * cubed * mean_k - inv_k * sum_du) / n_k
        dc2 = -0.5 * dr * cubed / n_k
        dc2 = pltpu.roll(dc2, 32, 1)
        pair = jnp.where(lanes < 32, dc1, jnp.where(lanes < 64, dc2, 0.0))
        answer = answer + (pltpu.roll(pair, 64, 1) if f else pair)
    dstat[pl.ds(tm, 1)] = answer.reshape(1, 1, 128)
    loop(GROUP, lambda d: first_copy(dstat, 2, d).start())

    def two_x(d):
        return pltpu.make_async_remote_copy(
            src_ref=sx2.at[lax.rem(y + d, ny)],
            dst_ref=rx2.at[d],
            send_sem=two_send.at[0, d],
            recv_sem=two_recv.at[0, d],
            device_id=at(tm, y_peer(d)),
            device_id_type=MESH,
        )

    def two_y(d):
        return pltpu.make_async_remote_copy(
            src_ref=sy2.at[lax.rem(x + d, NX)],
            dst_ref=ry2.at[d],
            send_sem=two_send.at[1, d],
            recv_sem=two_recv.at[1, d],
            device_id=at(x_peer(d)),
            device_id_type=MESH,
        )

    def three(d):
        return pltpu.make_async_remote_copy(
            src_ref=s3.at[lax.rem(z + d, nz)],
            dst_ref=r3.at[d],
            send_sem=three_send.at[d],
            recv_sem=three_recv.at[d],
            device_id=at(z_peer(d)),
            device_id_type=MESH,
        )

    loop(GROUP, lambda d: first_copy(dstat, 2, d).wait_recv())
    loop(nz, lambda d: second_copy(dstat, 3, d).start())

    for i in range(3):
        for d in range(1, NX):
            one_x(i, d).wait_recv()
    for p in range(4):
        rows = pl.ds(8 * p, 8)
        half = sx1[x, :, 16 * (p // 2) : 16 * (p // 2) + 16].astype(F32)
        for d in range(1, NX):
            half = half + rx1[d, :, 16 * (p // 2) : 16 * (p // 2) + 16].astype(F32)
        piece = half[:, 8 * (p % 2) : 8 * (p % 2) + 8]
        sx2[p] = piece.reshape(112, 256).astype(BF16)
    for d in (2, 1, 3):
        two_x(d).start()
    for i in range(3):
        for d in range(1, ny):
            one_y(i, d).wait_recv()
    for p in range(4):
        half = sy1[y, :, 16 * (p // 2) : 16 * (p // 2) + 16].astype(F32)
        for d in range(1, ny):
            half = half + ry1[d, :, 16 * (p // 2) : 16 * (p // 2) + 16].astype(F32)
        piece = half[:, 8 * (p % 2) : 8 * (p % 2) + 8].reshape(104, 256)
        sy2[p] = jnp.concatenate([piece, jnp.zeros((8, 256), F32)], axis=0).astype(BF16)
    for d in (2, 1, 3):
        two_y(d).start()

    loop(nz, lambda d: second_copy(dstat, 3, d).wait_recv())
    bounds = [(own + f, clip_end(starts, own + f, frames)) for f in range(2)]
    backs = masked_rows(dstat, bounds)
    back_one = spread(backs)
    back_two = spread(pltpu.roll(backs, 96, 1))
    for f in range(2):
        k = 2 + 2 * core + f
        values = xw[k].reshape(256, 256).astype(F32)
        result = (
            gwin[2 * core + f].reshape(256, 256).astype(F32)
            + da[f] * inv_rows[pl.ds(k, 1)]
            + back_one[f : f + 1]
            + values * (2.0 * back_two[f : f + 1])
        )
        grads_v[f] = result.reshape(16, 16, 256).astype(BF16)
    store_grads = pltpu.make_async_copy(grads_v, grads.at[0], store_sem.at[1])
    store_grads.start()

    for d in range(1, ny):
        two_x(d).wait_recv()
    summed = sx2[y].astype(F32)
    for d in range(1, ny):
        summed = summed + rx2[d].astype(F32)
    for h in range(2):
        total3[h, 0:112] = summed[:, 128 * h : 128 * h + 128]
    for d in range(1, NX):
        two_y(d).wait_recv()
    summed = sy2[x].astype(F32)
    for d in range(1, NX):
        summed = summed + ry2[d].astype(F32)
    for h in range(2):
        total3[h, 112:224] = summed[:, 128 * h : 128 * h + 128]
        total3[h, 224:256] = jnp.zeros((32, 128), F32)
        for q in range(nz):
            s3[q, :, 128 * h : 128 * h + 128] = total3[h, pl.ds(q, 32, stride=8)].astype(BF16)
    loop(nz, lambda d: three(d).start())
    loop(nz, lambda d: three(d).wait_recv())
    summed = s3[z].astype(F32)
    for d in range(1, nz):
        summed = summed + r3[d].astype(F32)
    summed = summed * scale
    for n in range(TAPS):
        i, lag, j = n // 9, n % 9 // 3, n % 3
        slot = n // 2 + 14 * (n % 2)
        to = 9 * lag + 3 * i + j
        wgrads[0, to : to + 1] = summed[slot : slot + 1]

    loop(GROUP, lambda d: first_copy(stat, 0, d).wait_send())
    loop(nz, lambda d: second_copy(stat, 1, d).wait_send())
    loop(GROUP, lambda d: first_copy(dstat, 2, d).wait_send())
    loop(nz, lambda d: second_copy(dstat, 3, d).wait_send())
    g_partner.wait_send()
    x_partner.wait_send()

    @pl.when(core == 0)
    def _():
        g_back[0].wait_send()
        g_back[1].wait_send()

    @pl.when(core == 1)
    def _():
        x_ahead.wait_send()

    for i in range(3):
        for d in range(1, 4):
            one_x(i, d).wait_send()
            one_y(i, d).wait_send()
    for d in range(1, 4):
        two_x(d).wait_send()
        two_y(d).wait_send()
    loop(nz, lambda d: three(d).wait_send())
    store_out.wait()
    store_grads.wait()


def local(nz, ny, scale, video_tile, clip_lengths, kernels, norm_gains, norm_shifts, cotangent):
    anywhere = pl.BlockSpec(memory_space=pl.ANY)
    vmem = pl.BlockSpec(memory_space=pltpu.VMEM)
    smem = pl.BlockSpec(memory_space=pltpu.SMEM)
    dma = pltpu.SemaphoreType.DMA
    return pl.pallas_call(
        functools.partial(kernel, nz, ny, scale),
        out_shape=(
            jax.ShapeDtypeStruct(video_tile.shape, BF16),
            jax.ShapeDtypeStruct(video_tile.shape, BF16),
            jax.ShapeDtypeStruct((1, TAPS, 256), F32),
        ),
        in_specs=[smem, vmem, vmem, anywhere, anywhere, anywhere],
        out_specs=(anywhere, anywhere, vmem),
        scratch_shapes=[
            pltpu.VMEM((6, 16, 16, 256), BF16),
            pltpu.VMEM((6, 16, 16, 256), BF16),
            pltpu.VMEM((3, 3, 3, 256, 256), BF16),
            pltpu.VMEM((6, 18, 16, 768), BF16),
            pltpu.VMEM((4, 18, 16, 768), BF16),
            pltpu.VMEM((6, 256, 256), BF16),
            pltpu.VMEM((384, 1536), BF16),
            pltpu.VMEM((nz * GROUP, 1, 128), F32),
            pltpu.VMEM((nz * GROUP, 1, 128), F32),
            pltpu.VMEM((8, 256), F32),
            pltpu.VMEM((8, 256), F32),
            pltpu.VMEM((8, 256), F32),
            pltpu.VMEM((2, 256, 256), F32),
            pltpu.VMEM((4, 14, 32, 256), BF16),
            pltpu.VMEM((4, 14, 32, 256), BF16),
            pltpu.VMEM((4, 13, 32, 256), BF16),
            pltpu.VMEM((4, 13, 32, 256), BF16),
            pltpu.VMEM((4, 112, 256), BF16),
            pltpu.VMEM((4, 112, 256), BF16),
            pltpu.VMEM((4, 112, 256), BF16),
            pltpu.VMEM((4, 112, 256), BF16),
            pltpu.VMEM((2, 256, 128), F32),
            pltpu.VMEM((8, 32, 256), BF16),
            pltpu.VMEM((8, 32, 256), BF16),
            pltpu.VMEM((2, 16, 16, 256), BF16),
            pltpu.VMEM((2, 16, 16, 256), BF16),
            dma((5,)),
            dma((5,)),
            dma((4,)),
            dma((4, 8)),
            dma((4, 8)),
            dma((2, 3, 4)),
            dma((2, 3, 4)),
            dma((2, 4)),
            dma((2, 4)),
            dma((8,)),
            dma((8,)),
            dma((2,)),
        ],
        compiler_params=pltpu.CompilerParams(
            collective_id=0, has_side_effects=True, vmem_limit_bytes=48 * 1024 * 1024
        ),
        cost_estimate=pl.CostEstimate(flops=5_500_000_000, bytes_accessed=5_000_000, transcendentals=400_000),
    )(clip_lengths, norm_gains, norm_shifts, video_tile, cotangent, kernels)


def solution(mesh):
    ny, tm = mesh.shape["dp"], mesh.shape["tm"]
    nz = tm // GROUP
    scale = 1.0 / math.sqrt(ny * tm * 2 * 256)
    placed = P("dp", "tm", None, None, None)
    return jax.shard_map(
        functools.partial(local, nz, ny, scale),
        mesh=mesh,
        in_specs=(placed, P("dp", None), P(), P(), P(), placed),
        out_specs=(placed, placed, P(None, None, ("dp", "tm"))),
        check_vma=False,
    )
```

time: 1770 us -> 56.3 us (0.03); the launches traced: 1750 us -> 56.1 us
  waiting for transfers between devices: 1160 us -> 0 us
  blocking collectives: 279 us -> 0 us
  local copies, waits for them, and re-layouts: 144 us -> 7.95 us
  loops' own time: 84.4 us -> 0 us
  Pallas kernels: 0 us -> 47.5 us
  other arithmetic: 27.2 us -> 0 us
  matrix products: 26 us -> 0 us
    reduce_scatter x1 -> x0, waiting for transfers between devices: 1160 us -> none  [reduce_terms(): lax.psum_scatter(terms, ('dp', 'tm'), scatter_dimension=1, tiled=True)]
    all_gather x4 -> x0, blocking collectives: 171 us -> none  [entering(): everything = jax.tree.map(lambda part: lax.all_gather(part, axis), shard)]
    unnamed x1 -> x0, blocking collectives: 108 us -> none
    another operation x2 -> x0, loops' own time: 84.4 us -> none  [entering(): return lax.fori_loop(0, devices, turn, start)]
    dynamic_slice x128 -> x0, local copies, waits for them, and re-layouts: 76.9 us -> none  [turn(): new = combine(before, jax.tree.map(lambda part: part[at], everything))]
    pallas_call x0 -> x1, Pallas kernels: none -> 47.5 us  [local(): pl.pallas_call(functools.partial(kernel, nz, ny, scale), out_shape=(jax.S...]
    dot_general x85 -> x0, matrix products: 26 us -> none  [the longest x27 10.1 us: taps_forward(): jnp.dot(sliced.reshape(-1, channels), kernel[delay_step, row_off, col_off...]
    concatenate x1 -> x0, local copies, waits for them, and re-layouts: 25.2 us -> none  [local(): jnp.concatenate(lag_parts, axis=0) * scale_factor]
  transfers between devices with their start and end apart: 3 -> 0, of which waited for: 1 -> 0; matrix products, arithmetic and copies ran while one was open for 7% -> 0% of each run, Pallas kernels for 0% -> 0%
where the time goes in v1:
time: 56.3 us; the launch traced here: 56.1 us
  Pallas kernels  47.5 us (84%)
  local copies, waits for them, and re-layouts  7.95 us (14%)
  between operations  0.65 us (1%)
    pallas_call x1, Pallas kernels, local(): pl.pallas_call(functools.partial(kernel, nz, ny, scale), out_shape=(jax.S...  47.5 us
    unnamed x14, local copies, waits for them, and re-layouts  7.31 us

profile of v1, /device:TPU:32, one launch (start us, length us, event | category | flops | bytes accessed | tf_op | source)
XLA Modules:
  0.0 56.1 jit_solution(13112369727898737968)
XLA Ops:
  0.6 0.0 copy-start
  0.6 2.0 %copy-done = bf16[1,3,3,3,256,256]{5,4,3,2,1,0:T(8,128)(2,1)S(1)} copy-done((bf16[1,3,3,3,256,256]{5,4,3,2,1,0:T(8,128)(2,1)S(1)}, bf16[1,3,3,3,256,256]{5,4,3,2,1,0:T(8,128)(2,1)}, u32[]{:S(2)}) %copy-start) | copy-done | bytes 3538968
  2.6 0.0 copy-start.1
  2.6 0.9 %copy-done.1 = bf16[1,2,16,16,256]{4,3,2,1,0:T(8,128)(2,1)S(1)} copy-done((bf16[1,2,16,16,256]{4,3,2,1,0:T(8,128)(2,1)S(1)}, bf16[1,2,16,16,256]{4,3,2,1,0:T(8,128)(2,1)}, u32[]{:S(2)}) %copy-start.1) | copy-done | bytes 262168
  3.6 0.0 copy-start.2
  3.6 0.9 %copy-done.2 = bf16[1,2,16,16,256]{4,3,2,1,0:T(8,128)(2,1)S(1)} copy-done((bf16[1,2,16,16,256]{4,3,2,1,0:T(8,128)(2,1)S(1)}, bf16[1,2,16,16,256]{4,3,2,1,0:T(8,128)(2,1)}, u32[]{:S(2)}) %copy-start.2) | copy-done | bytes 262168
  4.5 0.0 copy-start.3
  4.5 0.7 %copy-done.3 = f32[1,256]{1,0:T(1,128)S(1)} copy-done((f32[1,256]{1,0:T(1,128)S(1)}, f32[1,256]{1,0:T(1,128)}, u32[]{:S(2)}) %copy-start.3) | copy-done | bytes 1048
  5.2 0.0 copy-start.4
  5.2 0.7 %copy-done.4 = f32[1,256]{1,0:T(1,128)S(1)} copy-done((f32[1,256]{1,0:T(1,128)S(1)}, f32[1,256]{1,0:T(1,128)}, u32[]{:S(2)}) %copy-start.4) | copy-done | bytes 1048
  5.9 0.0 copy-start.5
  5.9 0.7 %copy-done.5 = s32[1,6]{1,0:T(1,128)S(1)} copy-done((s32[1,6]{1,0:T(1,128)S(1)}, s32[1,6]{1,0:T(1,128)}, u32[]{:S(2)}) %copy-start.5) | copy-done | bytes 48
  6.5 47.5 %shard_map.85 = (bf16[1,2,16,16,256]{4,3,2,1,0:T(8,128)(2,1)S(1)}, bf16[1,2,16,16,256]{4,3,2,1,0:T(8,128)(2,1)S(1)}, f32[1,27,256]{2,1,0:T(8,128)S(1)}) custom-call(s32[1,6]{1,0:T(1,128)S(1)} %copy-done.5, f32[1,256]{1,0:T(1,128)S(1)} %copy-done.3, f32[1,256]{1,0:T(1,128)S(1)} %copy-done.4, bf16[1,2,16,16,256]{4,3,2,1,0:T(8,128)(2,1)S(1)} %copy-done.1, ...), custom_call_target="tpu_custom_call" | custom-call | flops 5500000256 | bytes 5000000 | tf_op jit(solution)/shard_map/pallas_call | solution.py:612
  54.1 0.6 %copy.9 = f32[1,27,256]{2,0,1:T(1,128)} copy(f32[1,27,256]{2,1,0:T(8,128)S(1)} %get-tuple-element.5) | data formatting | bytes 55296 | tf_op jit(solution)/shard_map/pallas_call | solution.py:612
  54.7 0.7 %copy.12 = bf16[1,2,16,16,256]{4,3,2,1,0:T(8,128)(2,1)} copy(bf16[1,2,16,16,256]{4,3,2,1,0:T(8,128)(2,1)S(1)} %get-tuple-element.9) | data formatting | bytes 524288
  55.4 0.7 %copy.13 = bf16[1,2,16,16,256]{4,3,2,1,0:T(8,128)(2,1)} copy(bf16[1,2,16,16,256]{4,3,2,1,0:T(8,128)(2,1)S(1)} %get-tuple-element.10) | data formatting | bytes 524288
Async XLA Ops:
  0.6 2.0 %copy-start = (bf16[1,3,3,3,256,256]{5,4,3,2,1,0:T(8,128)(2,1)S(1)}, bf16[1,3,3,3,256,256]{5,4,3,2,1,0:T(8,128)(2,1)}, u32[]{:S(2)}) copy-start(bf16[1,3,3,3,256,256]{5,4,3,2,1,0:T(8,128)(2,1)} %kern.1) | copy-start | bytes 10616836
  2.6 0.9 %copy-start.1 = (bf16[1,2,16,16,256]{4,3,2,1,0:T(8,128)(2,1)S(1)}, bf16[1,2,16,16,256]{4,3,2,1,0:T(8,128)(2,1)}, u32[]{:S(2)}) copy-start(bf16[1,2,16,16,256]{4,3,2,1,0:T(8,128)(2,1)} %video.1) | copy-start | bytes 786436
  3.6 0.9 %copy-start.2 = (bf16[1,2,16,16,256]{4,3,2,1,0:T(8,128)(2,1)S(1)}, bf16[1,2,16,16,256]{4,3,2,1,0:T(8,128)(2,1)}, u32[]{:S(2)}) copy-start(bf16[1,2,16,16,256]{4,3,2,1,0:T(8,128)(2,1)} %cot.1) | copy-start | bytes 786436
  4.5 0.7 %copy-start.3 = (f32[1,256]{1,0:T(1,128)S(1)}, f32[1,256]{1,0:T(1,128)}, u32[]{:S(2)}) copy-start(f32[1,256]{1,0:T(1,128)} %gain.1) | copy-start | bytes 3076
  5.2 0.7 %copy-start.4 = (f32[1,256]{1,0:T(1,128)S(1)}, f32[1,256]{1,0:T(1,128)}, u32[]{:S(2)}) copy-start(f32[1,256]{1,0:T(1,128)} %shift.1) | copy-start | bytes 3076
  5.9 0.7 %copy-start.5 = (s32[1,6]{1,0:T(1,128)S(1)}, s32[1,6]{1,0:T(1,128)}, u32[]{:S(2)}) copy-start(s32[1,6]{1,0:T(1,128)} %lens.1) | copy-start | bytes 76

commit v2 on v1

v2 whole, which is shorter than its diff:
```python
import functools
import math

import jax
import jax.numpy as jnp
from jax import lax
from jax.experimental import pallas as pl
from jax.experimental.pallas import tpu as pltpu
from jax.sharding import PartitionSpec as P

EPS = 1e-05
NX = 4
NC = 2
GROUP = NX * NC
TAPS = 27
REACH = 12
MESH = pl.DeviceIdType.MESH
F32 = jnp.float32
BF16 = jnp.bfloat16
Z_TAPS = 5
PIECES = ((0, 2), (2, 4), (6, 5))
HALVES = ((0, 6), (6, 5))


def place_of(n):
    if n < Z_TAPS:
        return "z", n
    return "xy"[(n - Z_TAPS) % 2], (n - Z_TAPS) // 2


def iota(shape, dim):
    return lax.broadcasted_iota(jnp.int32, shape, dim)


def clip_begin(starts, t):
    begin = jnp.int32(0)
    for start in starts:
        begin = jnp.where(start <= t, start, begin)
    return begin


def clip_end(starts, t, frames):
    end = jnp.int32(frames)
    for start in reversed(starts):
        end = jnp.where(start > t, start, end)
    return end


def flag(condition):
    return jnp.where(condition, jnp.float32(1.0), jnp.float32(0.0))


def dot(a, b, contract=(1, 0), precision=None):
    return lax.dot_general(
        a,
        b,
        (((contract[0],), (contract[1],)), ((), ())),
        preferred_element_type=F32,
        precision=precision,
    )


def sigmoid(z):
    return 0.5 * jnp.tanh(0.5 * z) + 0.5


def pack_rows(rows):
    place = iota((8, 256), 0)
    stacked = jnp.zeros((8, 256), F32)
    for k, row in enumerate(rows):
        stacked = jnp.where(place == k, row, stacked)
    gather = ((iota((256, 128), 0) >> 3) == (iota((256, 128), 1) & 31)).astype(F32)
    grouped = dot(stacked, gather, precision=lax.Precision.HIGHEST)
    mine = (iota((8, 128), 1) >> 5) == iota((8, 128), 0)
    return jnp.sum(jnp.where(mine, grouped, 0.0), axis=0, keepdims=True)


def spread(rows):
    lanes = iota((8, 128), 1)
    clean = jnp.where(lanes < 32, rows, 0.0)
    matrix = (iota((128, 256), 0) == (iota((128, 256), 1) >> 3)).astype(F32)
    return dot(clean, matrix, precision=lax.Precision.HIGHEST)


def masked_rows(buffer, bounds):
    values = buffer[...]
    frame = 2 * iota(values.shape, 0) + (iota(values.shape, 2) >> 6)
    place = iota((8, 128), 0)
    rows = jnp.zeros((8, 128), F32)
    for k, (low, high) in enumerate(bounds):
        inside = (frame >= low) & (frame < high)
        total = jnp.sum(jnp.where(inside, values, 0.0), axis=0)
        rows = jnp.where(place == k, total, rows)
    return rows + pltpu.roll(rows, 64, 1)


def kernel(
    nz,
    ny,
    scale,
    lens_hbm,
    gain_hbm,
    shift_hbm,
    video,
    cot,
    kern,
    out,
    grads,
    wgrads,
    lens,
    gain,
    shift,
    xw,
    gwin,
    kv,
    gim,
    aim,
    act,
    lhs,
    stat,
    dstat,
    mean_rows,
    scale_rows,
    inv_rows,
    da,
    sx1,
    rx1,
    sy1,
    ry1,
    sz1,
    rz1,
    sx2,
    rx2,
    sy2,
    ry2,
    sz2,
    rz2,
    sz3,
    rz3,
    kx2,
    ky2,
    turn,
    total3,
    s3,
    r3,
    out_v,
    grads_v,
    load_sem,
    halo_send,
    halo_recv,
    chain_send,
    chain_recv,
    one_send,
    one_recv,
    two_send,
    two_recv,
    three_send,
    three_recv,
    store_sem,
):
    y = lax.axis_index("dp")
    tm = lax.axis_index("tm")
    core = lax.rem(tm, NC)
    x = lax.rem(tm // NC, NX)
    z = tm // GROUP
    within = lax.rem(tm, GROUP)
    chip = tm // NC
    chips = nz * NX
    frames = 2 * nz * GROUP
    base = 4 * chip
    own = 2 * tm

    def at(tm_index, dp_index=None):
        return {"dp": y if dp_index is None else dp_index, "tm": tm_index}

    def x_peer(d):
        return z * GROUP + lax.rem(x + d, NX) * NC + core

    def z_peer(d):
        return lax.rem(z + d, nz) * GROUP + within

    def y_peer(d):
        return lax.rem(y + d, ny)

    def chip_peer(d):
        return lax.rem(chip + d, chips) * NC + core

    partner = chip * NC + 1 - core

    beside = lax.rem(tm + 2 * core - 1 + 2 * chips, 2 * chips)

    stat[...] = jnp.zeros(stat.shape, F32)
    dstat[...] = jnp.zeros(dstat.shape, F32)

    load_x = pltpu.make_async_copy(video.at[0], xw.at[pl.ds(2 + 2 * core, 2)], load_sem.at[0])
    load_g = pltpu.make_async_copy(cot.at[0], gwin.at[pl.ds(2 * core, 2)], load_sem.at[1])
    load_k = [
        pltpu.make_async_copy(kern.at[0, lag], kv.at[lag], load_sem.at[2 + lag]) for lag in range(3)
    ]
    load_small = [
        pltpu.make_async_copy(src, dst, load_sem.at[5 + k])
        for k, (src, dst) in enumerate(((lens_hbm, lens), (gain_hbm, gain), (shift_hbm, shift)))
    ]
    load_x.start()
    load_g.start()
    for copy in load_small:
        copy.start()

    barrier = pltpu.get_barrier_semaphore()

    def greet(device):
        pl.semaphore_signal(barrier, inc=1, device_id=device, device_id_type=MESH)

    def greet_chips(d, carry):
        greet(at(chip_peer(d)))
        greet(at(chip_peer(chips - d)))
        return carry

    lax.fori_loop(1, REACH + 1, greet_chips, 0)
    far = range(REACH // NX + 1, nz - REACH // NX)
    for d in far:
        greet(at(z_peer(d)))
    for d in range(1, ny):
        greet(at(tm, y_peer(d)))
    greet(at(partner))
    greet(at(beside))
    for copy in load_k:
        copy.start()

    for copy in load_small:
        copy.wait()
    starts = []
    begin = jnp.int32(0)
    for k in range(6):
        starts.append(begin)
        begin = begin + lens[0, k]

    load_x.wait()
    sums = []
    for f in range(2):
        values = xw[2 + 2 * core + f].reshape(256, 256).astype(F32)
        sums.append(jnp.sum(values, axis=0, keepdims=True))
        sums.append(jnp.sum(values * values, axis=0, keepdims=True))
    stat[pl.ds(tm, 1)] = pack_rows(sums).reshape(1, 1, 128)

    pl.semaphore_wait(barrier, 2 * REACH + len(far) + (ny - 1) + 2)

    def first_copy(buffer, kind):
        mine = buffer.at[pl.ds(tm, 1)]
        return pltpu.make_async_remote_copy(
            src_ref=mine,
            dst_ref=mine,
            send_sem=chain_send.at[kind, 0],
            recv_sem=chain_recv.at[kind, 0],
            device_id=at(partner),
            device_id_type=MESH,
        )

    def second_copy(buffer, kind, d):
        mine = buffer.at[pl.ds(NC * chip, NC)]
        step = d if kind == 0 else chips - d
        return pltpu.make_async_remote_copy(
            src_ref=mine,
            dst_ref=mine,
            send_sem=chain_send.at[kind, d],
            recv_sem=chain_recv.at[kind, d],
            device_id=at(chip_peer(step)),
            device_id_type=MESH,
        )

    def loop(count, act_on):
        def body(d, carry):
            act_on(d)
            return carry

        lax.fori_loop(1, count, body, 0)

    first_copy(stat, 0).start()

    def halo(src, dst, sent, received, device):
        return pltpu.make_async_remote_copy(
            src_ref=src,
            dst_ref=dst,
            send_sem=halo_send.at[sent],
            recv_sem=halo_recv.at[received],
            device_id=at(device),
            device_id_type=MESH,
        )

    own_g = gwin.at[pl.ds(2 * core, 2)]
    own_x = xw.at[pl.ds(2 + 2 * core, 2)]
    after_g = gwin.at[pl.ds(4, 2)]
    g_partner = halo(cot.at[0], own_g, 0, 0, partner)
    x_partner = halo(video.at[0], own_x, 1, 1, partner)
    g_back = halo(cot.at[0], after_g, 2, 2, beside)
    g_relay = halo(after_g, after_g, 2, 2, partner)
    x_ahead = halo(video.at[0], xw.at[pl.ds(0, 2)], 3, 3, beside)
    g_partner.start()
    x_partner.start()

    pixel, source = iota((256, 256), 0), iota((256, 256), 1)
    right = ((source == pixel + 1) & ((pixel & 15) != 15)).astype(BF16)
    left = ((source == pixel - 1) & ((pixel & 15) != 0)).astype(BF16)
    both = jnp.concatenate([right, left], axis=0)

    def widen(target, k, values, first, last):
        shifted = dot(both, values).astype(BF16)
        target[k, 1:17, :, 256 * first : 256 * first + 256] = shifted[:256].reshape(16, 16, 256)
        target[k, 1:17, :, 256:512] = values.reshape(16, 16, 256)
        target[k, 1:17, :, 256 * last : 256 * last + 256] = shifted[256:].reshape(16, 16, 256)
        target[k, 0:1] = jnp.zeros((1, 16, 768), BF16)
        target[k, 17:18] = jnp.zeros((1, 16, 768), BF16)

    def backward(lag):
        taken = jnp.concatenate(
            [
                gim[pl.ds(2 * core + lag, 2), 2 - i : 18 - i].reshape(512, 768)
                for i in range(3)
            ],
            axis=1,
        )
        weights = jnp.concatenate(
            [kv[lag, i, j] for i in range(3) for j in range(3)], axis=1
        )
        part = dot(taken, weights, (1, 1))
        for f in range(2):
            piece = part[256 * f : 256 * f + 256]
            if lag == 0:
                da[f] = piece
            else:
                keep = flag(own + f + lag < clip_end(starts, own + f, frames))
                da[f] = da[f] + keep * piece

    def widen_g(v, carry):
        widen(gim, v, gwin[v].reshape(256, 256), 0, 2)
        return carry

    load_g.wait()
    lax.fori_loop(0, 2, lambda v, carry: widen_g(2 * core + v, carry), 0)

    first_copy(stat, 0).wait_recv()
    loop(REACH + 1, lambda d: second_copy(stat, 0, d).start())

    @pl.when(core == 0)
    def _():
        g_back.start()

    load_k[0].wait()
    backward(0)
    g_partner.wait_recv()
    lax.fori_loop(0, 2, lambda v, carry: widen_g(2 - 2 * core + v, carry), 0)

    bounds, counted = [], jnp.zeros((8, 128), F32)
    for k in range(6):
        t = base - 2 + k
        b = clip_begin(starts, t)
        bounds.append((b, t + 1))
        count = jnp.maximum(t + 1 - b, 1).astype(F32)
        counted = jnp.where(iota((8, 128), 0) == k, count, counted)
    counted = jnp.maximum(counted, 1.0) * 2048.0
    row, channel = iota((128, 256), 0), iota((128, 256), 1)
    wanted = 64 * ((row >> 3) & 3) + 8 * (row & 7) + 2 * (row >> 5) + core
    select = (channel == wanted).astype(BF16)
    blank = jnp.zeros((128, 256), BF16)
    for lag, v in ((0, 4), (0, 5), (1, 0), (1, 5), (2, 0), (2, 1)):
        lhs[128 * lag : 128 * lag + 128, 256 * v : 256 * v + 256] = blank

    loop(REACH + 1, lambda d: second_copy(stat, 0, d).wait_recv())

    @pl.when(core == 1)
    def _():
        x_ahead.start()

    averaged = masked_rows(stat, bounds) / counted
    squares = pltpu.roll(averaged, 96, 1)
    inv_std = lax.rsqrt(squares - averaged * averaged + EPS)
    mean_rows[...] = spread(averaged)
    wide_inv = spread(inv_std)
    inv_rows[...] = wide_inv
    scale_rows[...] = wide_inv * gain[...]

    def activate(k, carry):
        values = xw[k].reshape(256, 256).astype(F32)
        normed = (values - mean_rows[pl.ds(k, 1)]) * scale_rows[pl.ds(k, 1)] + shift[...]
        act[k] = (normed * sigmoid(normed)).astype(BF16)
        return carry

    x_partner.wait_recv()
    lax.fori_loop(2, 6, activate, 0)

    for u in range(4):
        turned = dot(select, act[2 + u], (1, 1))
        end = clip_end(starts, base + u, frames)
        for lag in range(3):
            masked = turned if lag == 0 else turned * flag(base + u + lag < end)
            v = u + lag
            lhs[128 * lag : 128 * lag + 128, 256 * v : 256 * v + 256] = masked.astype(BF16)

    @pl.when(core == 1)
    def _():
        g_back.wait_recv()
        g_relay.start()

    @pl.when(core == 0)
    def _():
        g_relay.wait_recv()

    lax.fori_loop(4, 6, widen_g, 0)

    def one_x(i, d):
        low, count = PIECES[i]
        target = lax.rem(x + d, NX)
        return pltpu.make_async_remote_copy(
            src_ref=sx1.at[target, pl.ds(low, count)],
            dst_ref=rx1.at[d, pl.ds(low, count)],
            send_sem=one_send.at[0, i, d],
            recv_sem=one_recv.at[0, i, d],
            device_id=at(x_peer(d)),
            device_id_type=MESH,
        )

    def one_y(i, d):
        low, count = PIECES[i]
        target = lax.rem(y + d, ny)
        return pltpu.make_async_remote_copy(
            src_ref=sy1.at[target, pl.ds(low, count)],
            dst_ref=ry1.at[d, pl.ds(low, count)],
            send_sem=one_send.at[1, i, d],
            recv_sem=one_recv.at[1, i, d],
            device_id=at(tm, y_peer(d)),
            device_id_type=MESH,
        )

    def one_z(d):
        return pltpu.make_async_remote_copy(
            src_ref=sz1.at[lax.rem(z + d, nz)],
            dst_ref=rz1.at[d],
            send_sem=three_send.at[2, d],
            recv_sem=three_recv.at[2, d],
            device_id=at(z_peer(d)),
            device_id_type=MESH,
        )

    def put_total(buffer, first, rows):
        for h in range(2):
            buffer[h, first : first + rows.shape[0]] = rows[:, 128 * h : 128 * h + 128]

    def every(buffer, start, count, stride):
        rows = [buffer[h, pl.ds(start, count, stride=stride)] for h in range(2)]
        return jnp.concatenate(rows, axis=1)

    for i in range(3):
        terms = dot(lhs[...], gim[:, 2 - i : 18 - i].reshape(1536, 768))
        for lag in range(3):
            for j in range(3):
                axis, slot = place_of(9 * i + 3 * lag + j)
                block = terms[128 * lag : 128 * lag + 128, 256 * j : 256 * j + 256]
                if axis == "z":
                    put_total(turn, 128 * slot, block)
                    for q in range(nz):
                        sz1[q, slot] = every(turn, 128 * slot + q, 16, 8).astype(BF16)
                    continue
                for p in range(4):
                    if axis == "x":
                        sx1[p, slot] = block[32 * p : 32 * p + 32].astype(BF16)
                    else:
                        rows = [block[32 * q + 8 * p : 32 * q + 8 * p + 8] for q in range(4)]
                        sy1[p, slot] = jnp.concatenate(rows, axis=0).astype(BF16)
        if i == 0:
            loop(nz, lambda d: one_z(d).start())
        for d in (2, 1, 3):
            one_x(i, d).start()
            one_y(i, d).start()

    for lag in (1, 2):
        load_k[lag].wait()
        backward(lag)

    lanes = iota((1, 128), 1)
    sums = []
    for f in range(2):
        k = 2 + 2 * core + f
        centred = xw[k].reshape(256, 256).astype(F32) - mean_rows[pl.ds(k, 1)]
        normed = centred * scale_rows[pl.ds(k, 1)] + shift[...]
        sig = sigmoid(normed)
        du = da[f] * (sig * (1.0 + normed * (1.0 - sig))) * gain[...]
        da[f] = du
        sums.append(jnp.sum(du, axis=0, keepdims=True))
        sums.append(jnp.sum(du * centred, axis=0, keepdims=True))
    packed = pack_rows(sums)
    row_of = iota((8, 128), 0)

    def pick(rows, k):
        return jnp.sum(jnp.where(row_of == k, rows, 0.0), axis=0, keepdims=True)

    answer = jnp.zeros((1, 128), F32)
    for f in range(2):
        k = 2 + 2 * core + f
        mean_k, inv_k, n_k = pick(averaged, k), pick(inv_std, k), pick(counted, k)
        sum_du = pltpu.roll(packed, 64, 1) if f else packed
        dr = pltpu.roll(sum_du, 96, 1)
        cubed = inv_k * inv_k * inv_k
        dc1 = (dr * cubed * mean_k - inv_k * sum_du) / n_k
        dc2 = -0.5 * dr * cubed / n_k
        dc2 = pltpu.roll(dc2, 32, 1)
        pair = jnp.where(lanes < 32, dc1, jnp.where(lanes < 64, dc2, 0.0))
        answer = answer + (pltpu.roll(pair, 64, 1) if f else pair)
    dstat[pl.ds(tm, 1)] = answer.reshape(1, 1, 128)
    first_copy(dstat, 1).start()

    @pl.when(core == 0)
    def _():
        x_ahead.wait_recv()
        lax.fori_loop(0, 2, activate, 0)

    def widen_a(k, carry):
        widen(aim, k, act[2 * core + k], 2, 0)
        return carry

    lax.fori_loop(0, 4, widen_a, 0)
    first_copy(dstat, 1).wait_recv()
    loop(REACH + 1, lambda d: second_copy(dstat, 1, d).start())
    for lag in range(3):
        taken = jnp.concatenate(
            [aim[2 - lag : 4 - lag, i : i + 16].reshape(512, 768) for i in range(3)], axis=1
        )
        part = dot(taken, kv[lag].reshape(2304, 256))
        for f in range(2):
            piece = part[256 * f : 256 * f + 256]
            if lag == 0:
                total = xw[2 + 2 * core + f].reshape(256, 256).astype(F32) + piece
            else:
                keep = flag(own + f - lag >= clip_begin(starts, own + f))
                total = total_f[f] + keep * piece
            if f == 0:
                first = total
            else:
                total_f = [first, total]
    for f in range(2):
        out_v[f] = total_f[f].reshape(16, 16, 256).astype(BF16)
    store_out = pltpu.make_async_copy(out_v, out.at[0], store_sem.at[0])
    store_out.start()

    def two(c, kind, d):
        mine, got = ((sx2, rx2), (sy2, ry2), (sz2, rz2), (sz3, rz3))[kind]
        along_y = kind in (0, 2)
        target = lax.rem(y + d, ny) if along_y else lax.rem(x + d, NX)
        src, dst = mine.at[target], got.at[d]
        if kind < 2:
            src, dst = src.at[pl.ds(48 * c, 48)], dst.at[pl.ds(48 * c, 48)]
        return pltpu.make_async_remote_copy(
            src_ref=src,
            dst_ref=dst,
            send_sem=two_send.at[kind, c, d],
            recv_sem=two_recv.at[kind, c, d],
            device_id=at(tm, y_peer(d)) if along_y else at(x_peer(d)),
            device_id_type=MESH,
        )

    def three(c, d):
        return pltpu.make_async_remote_copy(
            src_ref=s3.at[lax.rem(z + d, nz), pl.ds(16 * c, 16)],
            dst_ref=r3.at[d, pl.ds(16 * c, 16)],
            send_sem=three_send.at[c, d],
            recv_sem=three_recv.at[c, d],
            device_id=at(z_peer(d)),
            device_id_type=MESH,
        )

    total3[...] = jnp.zeros(total3.shape, F32)

    def gathered(c, mine, got, keep, staged, me):
        low, count = HALVES[c]
        first = 48 * c
        for p in range(4):
            some = pl.ds(16 * (p // 2), 16)
            half = mine[me, pl.ds(low, count), some].astype(F32)
            for d in range(1, 4):
                half = half + got[d, pl.ds(low, count), some].astype(F32)
            piece = half[:, 8 * (p % 2) : 8 * (p % 2) + 8].reshape(8 * count, 256)
            if 8 * count < 48:
                piece = jnp.concatenate([piece, jnp.zeros((48 - 8 * count, 256), F32)], axis=0)
            keep[p, first : first + 48] = piece
            staged[p, first : first + 48] = piece.astype(BF16)

    def to_two(c):
        pieces = (0, 1) if c == 0 else (2,)
        for kind, one, mine, got, keep, staged, me in (
            (0, one_x, sx1, rx1, kx2, sx2, x),
            (1, one_y, sy1, ry1, ky2, sy2, y),
        ):
            for i in pieces:
                for d in range(1, 4):
                    one(i, d).wait_recv()
            gathered(c, mine, got, keep, staged, me)
            for d in (2, 1, 3):
                two(c, kind, d).start()

    def to_three(c):
        some = pl.ds(48 * c, 48)
        for kind, keep, got, me in ((0, kx2, rx2, y), (1, ky2, ry2, x)):
            for d in range(1, 4):
                two(c, kind, d).wait_recv()
            total = keep[me, some]
            for d in range(1, 4):
                total = total + got[d, some].astype(F32)
            put_total(total3, 128 * c + 48 * kind, total)
        for q in range(nz):
            s3[q, 16 * c : 16 * c + 16] = every(total3, 128 * c + q, 16, 8).astype(BF16)
        loop(nz, lambda d: three(c, d).start())

    def finish(rows, taps):
        for n in range(TAPS):
            if place_of(n) in taps:
                k = taps.index(place_of(n))
                to = 9 * (n % 9 // 3) + 3 * (n // 9) + n % 3
                wgrads[to] = rows[k : k + 1] * scale

    to_two(0)
    to_two(1)

    loop(nz, lambda d: one_z(d).wait_recv())
    total = sz1[z].astype(F32)
    for d in range(1, nz):
        total = total + rz1[d].astype(F32)
    put_total(turn, 0, total.reshape(16 * Z_TAPS, 256))
    for p in range(4):
        sz2[p] = every(turn, p, 32, 4).astype(BF16)
    for d in (2, 1, 3):
        two(0, 2, d).start()

    to_three(0)
    to_three(1)

    for d in (1, 2, 3):
        two(0, 2, d).wait_recv()
    total = every(turn, y, 32, 4)
    for d in range(1, 4):
        total = total + rz2[d].astype(F32)
    put_total(turn, 128, total)
    for p in range(4):
        sz3[p] = every(turn, 128 + p, 16, 4).astype(BF16)
    for d in (2, 1, 3):
        two(0, 3, d).start()

    loop(REACH + 1, lambda d: second_copy(dstat, 1, d).wait_recv())
    bounds = [(own + f, clip_end(starts, own + f, frames)) for f in range(2)]
    backs = masked_rows(dstat, bounds)
    back_one = spread(backs)
    back_two = spread(pltpu.roll(backs, 96, 1))
    for f in range(2):
        k = 2 + 2 * core + f
        values = xw[k].reshape(256, 256).astype(F32)
        result = (
            gwin[2 * core + f].reshape(256, 256).astype(F32)
            + da[f] * inv_rows[pl.ds(k, 1)]
            + back_one[f : f + 1]
            + values * (2.0 * back_two[f : f + 1])
        )
        grads_v[f] = result.reshape(16, 16, 256).astype(BF16)
    store_grads = pltpu.make_async_copy(grads_v, grads.at[0], store_sem.at[1])
    store_grads.start()

    for c in range(2):
        loop(nz, lambda d: three(c, d).wait_recv())
        total = every(total3, 128 * c + z, 16, 8)
        for d in range(1, nz):
            total = total + r3[d, pl.ds(16 * c, 16)].astype(F32)
        low, count = HALVES[c]
        finish(total, [(axis, low + k) for axis in "xy" for k in range(6)])
    for d in (1, 2, 3):
        two(0, 3, d).wait_recv()
    total = every(turn, 128 + x, 16, 4)
    for d in range(1, 4):
        total = total + rz3[d].astype(F32)
    finish(total, [("z", k) for k in range(Z_TAPS)])

    first_copy(stat, 0).wait_send()
    loop(REACH + 1, lambda d: second_copy(stat, 0, d).wait_send())
    first_copy(dstat, 1).wait_send()
    loop(REACH + 1, lambda d: second_copy(dstat, 1, d).wait_send())
    g_partner.wait_send()
    x_partner.wait_send()

    x_or_g = ((g_back, 0), (g_relay, 1), (x_ahead, 1))
    for copy, sender in x_or_g:
        pl.when(core == sender)(copy.wait_send)
    for d in range(1, 4):
        for i in range(3):
            one_x(i, d).wait_send()
            one_y(i, d).wait_send()
        for c, kind in ((0, 0), (0, 1), (1, 0), (1, 1), (0, 2), (0, 3)):
            two(c, kind, d).wait_send()
    loop(nz, lambda d: one_z(d).wait_send())
    for c in range(2):
        loop(nz, lambda d: three(c, d).wait_send())
    store_out.wait()
    store_grads.wait()


def hand_over(*refs):
    sources, targets, held, sems = refs[:3], refs[3:6], refs[6:9], refs[9]
    into = [pltpu.make_async_copy(sources[k], held[k], sems.at[0, k]) for k in range(3)]
    out = [pltpu.make_async_copy(held[k], targets[k], sems.at[1, k]) for k in range(3)]
    for copy in into:
        copy.start()
    for k in range(3):
        into[k].wait()
        out[k].start()
    for copy in out:
        copy.wait()


def local(nz, ny, scale, video_tile, clip_lengths, kernels, norm_gains, norm_shifts, cotangent):
    hbm = pl.BlockSpec(memory_space=pltpu.HBM)
    vmem = pl.BlockSpec(memory_space=pltpu.VMEM)
    dma = pltpu.SemaphoreType.DMA
    made = pl.pallas_call(
        functools.partial(kernel, nz, ny, scale),
        out_shape=(
            jax.ShapeDtypeStruct(video_tile.shape, BF16),
            jax.ShapeDtypeStruct(video_tile.shape, BF16),
            jax.ShapeDtypeStruct((TAPS, 1, 256), F32),
        ),
        in_specs=[hbm] * 6,
        out_specs=(hbm, hbm, vmem),
        scratch_shapes=[
            pltpu.SMEM((1, 6), jnp.int32),
            pltpu.VMEM((1, 256), F32),
            pltpu.VMEM((1, 256), F32),
            pltpu.VMEM((6, 16, 16, 256), BF16),
            pltpu.VMEM((6, 16, 16, 256), BF16),
            pltpu.VMEM((3, 3, 3, 256, 256), BF16),
            pltpu.VMEM((6, 18, 16, 768), BF16),
            pltpu.VMEM((4, 18, 16, 768), BF16),
            pltpu.VMEM((6, 256, 256), BF16),
            pltpu.VMEM((384, 1536), BF16),
            pltpu.VMEM((nz * GROUP, 1, 128), F32),
            pltpu.VMEM((nz * GROUP, 1, 128), F32),
            pltpu.VMEM((8, 256), F32),
            pltpu.VMEM((8, 256), F32),
            pltpu.VMEM((8, 256), F32),
            pltpu.VMEM((2, 256, 256), F32),
            pltpu.VMEM((4, 11, 32, 256), BF16),
            pltpu.VMEM((4, 11, 32, 256), BF16),
            pltpu.VMEM((4, 11, 32, 256), BF16),
            pltpu.VMEM((4, 11, 32, 256), BF16),
            pltpu.VMEM((8, Z_TAPS, 16, 256), BF16),
            pltpu.VMEM((8, Z_TAPS, 16, 256), BF16),
            pltpu.VMEM((4, 96, 256), BF16),
            pltpu.VMEM((4, 96, 256), BF16),
            pltpu.VMEM((4, 96, 256), BF16),
            pltpu.VMEM((4, 96, 256), BF16),
            pltpu.VMEM((4, 32, 256), BF16),
            pltpu.VMEM((4, 32, 256), BF16),
            pltpu.VMEM((4, 16, 256), BF16),
            pltpu.VMEM((4, 16, 256), BF16),
            pltpu.VMEM((4, 96, 256), F32),
            pltpu.VMEM((4, 96, 256), F32),
            pltpu.VMEM((2, 128 * Z_TAPS, 128), F32),
            pltpu.VMEM((2, 256, 128), F32),
            pltpu.VMEM((8, 32, 256), BF16),
            pltpu.VMEM((8, 32, 256), BF16),
            pltpu.VMEM((2, 16, 16, 256), BF16),
            pltpu.VMEM((2, 16, 16, 256), BF16),
            dma((8,)),
            dma((4,)),
            dma((4,)),
            dma((2, REACH + 1)),
            dma((2, REACH + 1)),
            dma((2, 3, 4)),
            dma((2, 3, 4)),
            dma((4, 2, 4)),
            dma((4, 2, 4)),
            dma((3, 8)),
            dma((3, 8)),
            dma((2,)),
        ],
        compiler_params=pltpu.CompilerParams(
            collective_id=0, has_side_effects=True, vmem_limit_bytes=60 * 1024 * 1024
        ),
        cost_estimate=pl.CostEstimate(flops=5_500_000_000, bytes_accessed=5_000_000, transcendentals=400_000),
    )(clip_lengths, norm_gains, norm_shifts, video_tile, cotangent, kernels)
    results = pl.pallas_call(
        hand_over,
        out_shape=tuple(jax.ShapeDtypeStruct(part.shape, part.dtype) for part in made),
        in_specs=[hbm] * 3,
        out_specs=(hbm,) * 3,
        scratch_shapes=[pltpu.VMEM(part.shape, part.dtype) for part in made] + [dma((2, 3))],
        compiler_params=pltpu.CompilerParams(vmem_limit_bytes=60 * 1024 * 1024),
    )(*made)
    return (results[0], results[1], results[2].transpose(1, 0, 2))


def solution(mesh):
    ny, tm = mesh.shape["dp"], mesh.shape["tm"]
    nz = tm // GROUP
    scale = 1.0 / math.sqrt(ny * tm * 2 * 256)
    placed = P("dp", "tm", None, None, None)
    return jax.shard_map(
        functools.partial(local, nz, ny, scale),
        mesh=mesh,
        in_specs=(placed, P("dp", None), P(), P(), P(), placed),
        out_specs=(placed, placed, P(None, None, ("dp", "tm"))),
        check_vma=False,
    )
```

time: 56.3 us -> 45.1 us (0.80)
  local copies, waits for them, and re-layouts: 7.95 us -> 0 us
  Pallas kernels: 47.5 us -> 44 us
    unnamed x14 -> x0, local copies, waits for them, and re-layouts: 7.31 us -> none
    pallas_call x1, Pallas kernels: 47.5 us -> 42.2 us  [local(): pl.pallas_call(functools.partial(kernel, nz, ny, scale), out_shape=(jax.S...]
    pallas_call x0 -> x1, Pallas kernels: none -> 1.79 us  [local(): pl.pallas_call(hand_over, out_shape=tuple((jax.ShapeDtypeStruct(part.shap...]
    pallas_call x1 -> x0, local copies, waits for them, and re-layouts: 0.64 us -> none  [local(): pl.pallas_call(functools.partial(kernel, nz, ny, scale), out_shape=(jax.S...]
where the time goes in v2:
time: 45.1 us; the launch traced here: 44.7 us
  Pallas kernels  44 us (98%)
  between operations  0.64 us (1%)
    pallas_call x1, Pallas kernels, local(): pl.pallas_call(functools.partial(kernel, nz, ny, scale), out_shape=(jax.S...  42.2 us
    pallas_call x1, Pallas kernels, local(): pl.pallas_call(hand_over, out_shape=tuple((jax.ShapeDtypeStruct(part.shap...  1.79 us

profile of v2, /device:TPU:32, one launch (start us, length us, event | category | flops | bytes accessed | tf_op | source)
XLA Modules:
  0.0 44.7 jit_solution(16891185869412758646)
XLA Ops:
  0.6 42.2 %shard_map.85 = (bf16[1,2,16,16,256]{4,3,2,1,0:T(8,128)(2,1)}, bf16[1,2,16,16,256]{4,3,2,1,0:T(8,128)(2,1)}, f32[27,1,256]{2,1,0:T(1,128)}) custom-call(s32[1,6]{1,0:T(1,128)} %lens_hbm.1, f32[1,256]{1,0:T(1,128)} %gain_hbm.1, f32[1,256]{1,0:T(1,128)} %shift_hbm.1, bf16[1,2,16,16,256]{4,3,2,1,0:T(8,128)(2,1)} %video.1, bf16[1,2,16,16,256]{4,3,2,1,0:T(8,128)(2,1)} %cot.1, ...), custom_call_target="tpu_custom_call" | custom-call | flops 5500000256 | bytes 5000000 | tf_op jit(solution)/shard_map/pallas_call | solution.py:718
  42.9 1.8 %shard_map.86 = (bf16[1,2,16,16,256]{4,3,2,1,0:T(8,128)(2,1)}, bf16[1,2,16,16,256]{4,3,2,1,0:T(8,128)(2,1)}, f32[27,1,256]{2,1,0:T(1,128)}) custom-call(bf16[1,2,16,16,256]{4,3,2,1,0:T(8,128)(2,1)} %get-tuple-element.9.refs_0_, bf16[1,2,16,16,256]{4,3,2,1,0:T(8,128)(2,1)} %get-tuple-element.10.refs_1_, f32[27,1,256]{2,1,0:T(1,128)} %get-tuple-element.11.refs_2_), custom_call_target="tpu_custom_call" | custom-call | tf_op jit(solution)/shard_map/pallas_call | solution.py:784

commit v3 on v2

--- a/solution.py
+++ b/solution.py
@@ -18,14 +18,17 @@
 F32 = jnp.float32
 BF16 = jnp.bfloat16
 Z_TAPS = 5
-PIECES = ((0, 2), (2, 4), (6, 5))
-HALVES = ((0, 6), (6, 5))
+Z_PIECES = {1: (0, 2), 4: (2, 3)}
+PIECES = {0: (0, 1), 2: (1, 2), 4: (3, 2), 6: (5, 3), 8: (8, 3)}
+HALVES = ((0, 8, 0, 64), (8, 3, 64, 32))
 
 
 def place_of(n):
-    if n < Z_TAPS:
-        return "z", n
-    return "xy"[(n - Z_TAPS) % 2], (n - Z_TAPS) // 2
+    step, lag = n // 3, n % 3
+    if step < Z_TAPS:
+        return ("xyz"[lag], step)
+    k = n - Z_TAPS
+    return "xy"[k % 2], k // 2
 
 
 def iota(shape, dim):
@@ -75,11 +78,12 @@
     return jnp.sum(jnp.where(mine, grouped, 0.0), axis=0, keepdims=True)
 
 
-def spread(rows):
-    lanes = iota((8, 128), 1)
-    clean = jnp.where(lanes < 32, rows, 0.0)
+def spread(*parts):
+    rows = jnp.concatenate(parts, axis=0)
+    clean = jnp.where(iota(rows.shape, 1) < 32, rows, 0.0)
     matrix = (iota((128, 256), 0) == (iota((128, 256), 1) >> 3)).astype(F32)
-    return dot(clean, matrix, precision=lax.Precision.HIGHEST)
+    wide = dot(clean, matrix, precision=lax.Precision.HIGHEST)
+    return [wide[8 * k : 8 * k + 8] for k in range(len(parts))]
 
 
 def masked_rows(buffer, bounds):
@@ -97,7 +101,6 @@
 def kernel(
     nz,
     ny,
-    scale,
     lens_hbm,
     gain_hbm,
     shift_hbm,
@@ -106,7 +109,9 @@
     kern,
     out,
     grads,
-    wgrads,
+    own3,
+    r3,
+    rz3,
     lens,
     gain,
     shift,
@@ -136,13 +141,12 @@
     sz2,
     rz2,
     sz3,
-    rz3,
     kx2,
     ky2,
     turn,
     total3,
     s3,
-    r3,
+    own_v,
     out_v,
     grads_v,
     load_sem,
@@ -216,12 +220,12 @@
         greet(at(chip_peer(chips - d)))
         return carry
 
-    lax.fori_loop(1, REACH + 1, greet_chips, 0)
     far = range(REACH // NX + 1, nz - REACH // NX)
     for d in far:
         greet(at(z_peer(d)))
     for d in range(1, ny):
         greet(at(tm, y_peer(d)))
+    lax.fori_loop(0, REACH, lambda d, carry: greet_chips(REACH - d, carry), 0)
     greet(at(partner))
     greet(at(beside))
     for copy in load_k:
@@ -289,12 +293,11 @@
 
     own_g = gwin.at[pl.ds(2 * core, 2)]
     own_x = xw.at[pl.ds(2 + 2 * core, 2)]
-    after_g = gwin.at[pl.ds(4, 2)]
     g_partner = halo(cot.at[0], own_g, 0, 0, partner)
     x_partner = halo(video.at[0], own_x, 1, 1, partner)
-    g_back = halo(cot.at[0], after_g, 2, 2, beside)
-    g_relay = halo(after_g, after_g, 2, 2, partner)
-    x_ahead = halo(video.at[0], xw.at[pl.ds(0, 2)], 3, 3, beside)
+    g_back = [halo(cot.at[0, f], gwin.at[4 + f], 2 + f, 2 + f, beside) for f in range(2)]
+    g_relay = [halo(gwin.at[4 + f], gwin.at[4 + f], 2 + f, 2 + f, partner) for f in range(2)]
+    x_ahead = halo(video.at[0], xw.at[pl.ds(0, 2)], 4, 4, beside)
     g_partner.start()
     x_partner.start()
 
@@ -339,11 +342,12 @@
     lax.fori_loop(0, 2, lambda v, carry: widen_g(2 * core + v, carry), 0)
 
     first_copy(stat, 0).wait_recv()
-    loop(REACH + 1, lambda d: second_copy(stat, 0, d).start())
+    loop(REACH + 1, lambda d: second_copy(stat, 0, REACH + 1 - d).start())
 
     @pl.when(core == 0)
     def _():
-        g_back.start()
+        g_back[0].start()
+        g_back[1].start()
 
     load_k[0].wait()
     backward(0)
@@ -374,8 +378,8 @@
     averaged = masked_rows(stat, bounds) / counted
     squares = pltpu.roll(averaged, 96, 1)
     inv_std = lax.rsqrt(squares - averaged * averaged + EPS)
-    mean_rows[...] = spread(averaged)
-    wide_inv = spread(inv_std)
+    wide_mean, wide_inv = spread(averaged, inv_std)
+    mean_rows[...] = wide_mean
     inv_rows[...] = wide_inv
     scale_rows[...] = wide_inv * gain[...]
 
@@ -386,9 +390,9 @@
         return carry
 
     x_partner.wait_recv()
-    lax.fori_loop(2, 6, activate, 0)
 
     for u in range(4):
+        activate(2 + u, 0)
         turned = dot(select, act[2 + u], (1, 1))
         end = clip_end(starts, base + u, frames)
         for lag in range(3):
@@ -396,16 +400,18 @@
             v = u + lag
             lhs[128 * lag : 128 * lag + 128, 256 * v : 256 * v + 256] = masked.astype(BF16)
 
-    @pl.when(core == 1)
-    def _():
-        g_back.wait_recv()
-        g_relay.start()
-
-    @pl.when(core == 0)
-    def _():
-        g_relay.wait_recv()
-
-    lax.fori_loop(4, 6, widen_g, 0)
+    for f in range(2):
+
+        @pl.when(core == 1)
+        def _():
+            g_back[f].wait_recv()
+            g_relay[f].start()
+
+        @pl.when(core == 0)
+        def _():
+            g_relay[f].wait_recv()
+
+        widen_g(4 + f, 0)
 
     def one_x(i, d):
         low, count = PIECES[i]
@@ -413,8 +419,8 @@
         return pltpu.make_async_remote_copy(
             src_ref=sx1.at[target, pl.ds(low, count)],
             dst_ref=rx1.at[d, pl.ds(low, count)],
-            send_sem=one_send.at[0, i, d],
-            recv_sem=one_recv.at[0, i, d],
+            send_sem=one_send.at[0, i // 2, d],
+            recv_sem=one_recv.at[0, i // 2, d],
             device_id=at(x_peer(d)),
             device_id_type=MESH,
         )
@@ -425,18 +431,19 @@
         return pltpu.make_async_remote_copy(
             src_ref=sy1.at[target, pl.ds(low, count)],
             dst_ref=ry1.at[d, pl.ds(low, count)],
-            send_sem=one_send.at[1, i, d],
-            recv_sem=one_recv.at[1, i, d],
+            send_sem=one_send.at[1, i // 2, d],
+            recv_sem=one_recv.at[1, i // 2, d],
             device_id=at(tm, y_peer(d)),
             device_id_type=MESH,
         )
 
-    def one_z(d):
+    def one_z(i, d):
+        low, count = Z_PIECES[i]
         return pltpu.make_async_remote_copy(
-            src_ref=sz1.at[lax.rem(z + d, nz)],
-            dst_ref=rz1.at[d],
-            send_sem=three_send.at[2, d],
-            recv_sem=three_recv.at[2, d],
+            src_ref=sz1.at[lax.rem(z + d, nz), pl.ds(low, count)],
+            dst_ref=rz1.at[d, pl.ds(low, count)],
+            send_sem=three_send.at[2 + i // 4, d],
+            recv_sem=three_recv.at[2 + i // 4, d],
             device_id=at(z_peer(d)),
             device_id_type=MESH,
         )
@@ -449,28 +456,29 @@
         rows = [buffer[h, pl.ds(start, count, stride=stride)] for h in range(2)]
         return jnp.concatenate(rows, axis=1)
 
-    for i in range(3):
-        terms = dot(lhs[...], gim[:, 2 - i : 18 - i].reshape(1536, 768))
+    for step in range(9):
+        i, j = step // 3, step % 3
+        terms = dot(lhs[...], gim[:, 2 - i : 18 - i, :, 256 * j : 256 * j + 256].reshape(1536, 256))
         for lag in range(3):
-            for j in range(3):
-                axis, slot = place_of(9 * i + 3 * lag + j)
-                block = terms[128 * lag : 128 * lag + 128, 256 * j : 256 * j + 256]
-                if axis == "z":
-                    put_total(turn, 128 * slot, block)
-                    for q in range(nz):
-                        sz1[q, slot] = every(turn, 128 * slot + q, 16, 8).astype(BF16)
-                    continue
-                for p in range(4):
-                    if axis == "x":
-                        sx1[p, slot] = block[32 * p : 32 * p + 32].astype(BF16)
-                    else:
-                        rows = [block[32 * q + 8 * p : 32 * q + 8 * p + 8] for q in range(4)]
-                        sy1[p, slot] = jnp.concatenate(rows, axis=0).astype(BF16)
-        if i == 0:
-            loop(nz, lambda d: one_z(d).start())
-        for d in (2, 1, 3):
-            one_x(i, d).start()
-            one_y(i, d).start()
+            axis, slot = place_of(3 * step + lag)
+            block = terms[128 * lag : 128 * lag + 128]
+            if axis == "z":
+                put_total(turn, 128 * slot, block)
+                for q in range(nz):
+                    sz1[q, slot] = every(turn, 128 * slot + q, 16, 8).astype(BF16)
+                continue
+            for p in range(4):
+                if axis == "x":
+                    sx1[p, slot] = block[32 * p : 32 * p + 32].astype(BF16)
+                else:
+                    rows = [block[32 * q + 8 * p : 32 * q + 8 * p + 8] for q in range(4)]
+                    sy1[p, slot] = jnp.concatenate(rows, axis=0).astype(BF16)
+        if step in PIECES:
+            for d in (2, 1, 3):
+                one_x(step, d).start()
+                one_y(step, d).start()
+        if step in Z_PIECES:
+            loop(nz, lambda d: one_z(step, d).start())
 
     for lag in (1, 2):
         load_k[lag].wait()
@@ -518,8 +526,6 @@
         return carry
 
     lax.fori_loop(0, 4, widen_a, 0)
-    first_copy(dstat, 1).wait_recv()
-    loop(REACH + 1, lambda d: second_copy(dstat, 1, d).start())
     for lag in range(3):
         taken = jnp.concatenate(
             [aim[2 - lag : 4 - lag, i : i + 16].reshape(512, 768) for i in range(3)], axis=1
@@ -547,7 +553,8 @@
         target = lax.rem(y + d, ny) if along_y else lax.rem(x + d, NX)
         src, dst = mine.at[target], got.at[d]
         if kind < 2:
-            src, dst = src.at[pl.ds(48 * c, 48)], dst.at[pl.ds(48 * c, 48)]
+            some = pl.ds(HALVES[c][2], HALVES[c][3])
+            src, dst = src.at[some], dst.at[some]
         return pltpu.make_async_remote_copy(
             src_ref=src,
             dst_ref=dst,
@@ -570,21 +577,22 @@
     total3[...] = jnp.zeros(total3.shape, F32)
 
     def gathered(c, mine, got, keep, staged, me):
-        low, count = HALVES[c]
-        first = 48 * c
-        for p in range(4):
-            some = pl.ds(16 * (p // 2), 16)
+        low, count, first, length = HALVES[c]
+        for both_p in range(2):
+            some = pl.ds(16 * both_p, 16)
             half = mine[me, pl.ds(low, count), some].astype(F32)
             for d in range(1, 4):
                 half = half + got[d, pl.ds(low, count), some].astype(F32)
-            piece = half[:, 8 * (p % 2) : 8 * (p % 2) + 8].reshape(8 * count, 256)
-            if 8 * count < 48:
-                piece = jnp.concatenate([piece, jnp.zeros((48 - 8 * count, 256), F32)], axis=0)
-            keep[p, first : first + 48] = piece
-            staged[p, first : first + 48] = piece.astype(BF16)
+            for p in (2 * both_p, 2 * both_p + 1):
+                piece = half[:, 8 * (p % 2) : 8 * (p % 2) + 8].reshape(8 * count, 256)
+                if 8 * count < length:
+                    blank = jnp.zeros((length - 8 * count, 256), F32)
+                    piece = jnp.concatenate([piece, blank], axis=0)
+                keep[p, first : first + length] = piece
+                staged[p, first : first + length] = piece.astype(BF16)
 
     def to_two(c):
-        pieces = (0, 1) if c == 0 else (2,)
+        pieces = (0, 2, 4, 6) if c == 0 else (8,)
         for kind, one, mine, got, keep, staged, me in (
             (0, one_x, sx1, rx1, kx2, sx2, x),
             (1, one_y, sy1, ry1, ky2, sy2, y),
@@ -597,29 +605,25 @@
                 two(c, kind, d).start()
 
     def to_three(c):
-        some = pl.ds(48 * c, 48)
+        low, count, first, length = HALVES[c]
+        some = pl.ds(first, length)
         for kind, keep, got, me in ((0, kx2, rx2, y), (1, ky2, ry2, x)):
             for d in range(1, 4):
                 two(c, kind, d).wait_recv()
             total = keep[me, some]
             for d in range(1, 4):
                 total = total + got[d, some].astype(F32)
-            put_total(total3, 128 * c + 48 * kind, total)
+            put_total(total3, 128 * c + length * kind, total)
         for q in range(nz):
             s3[q, 16 * c : 16 * c + 16] = every(total3, 128 * c + q, 16, 8).astype(BF16)
-        loop(nz, lambda d: three(c, d).start())
-
-    def finish(rows, taps):
-        for n in range(TAPS):
-            if place_of(n) in taps:
-                k = taps.index(place_of(n))
-                to = 9 * (n % 9 // 3) + 3 * (n // 9) + n % 3
-                wgrads[to] = rows[k : k + 1] * scale
+        for d in sorted(range(1, nz), key=lambda d: -min(d, nz - d)):
+            three(c, d).start()
 
     to_two(0)
     to_two(1)
 
-    loop(nz, lambda d: one_z(d).wait_recv())
+    for i in Z_PIECES:
+        loop(nz, lambda d: one_z(i, d).wait_recv())
     total = sz1[z].astype(F32)
     for d in range(1, nz):
         total = total + rz1[d].astype(F32)
@@ -629,6 +633,8 @@
     for d in (2, 1, 3):
         two(0, 2, d).start()
 
+    first_copy(dstat, 1).wait_recv()
+    loop(REACH + 1, lambda d: second_copy(dstat, 1, d).start())
     to_three(0)
     to_three(1)
 
@@ -646,8 +652,7 @@
     loop(REACH + 1, lambda d: second_copy(dstat, 1, d).wait_recv())
     bounds = [(own + f, clip_end(starts, own + f, frames)) for f in range(2)]
     backs = masked_rows(dstat, bounds)
-    back_one = spread(backs)
-    back_two = spread(pltpu.roll(backs, 96, 1))
+    back_one, back_two = spread(backs, pltpu.roll(backs, 96, 1))
     for f in range(2):
         k = 2 + 2 * core + f
         values = xw[k].reshape(256, 256).astype(F32)
@@ -662,68 +667,101 @@
     store_grads.start()
 
     for c in range(2):
+        own_v[16 * c : 16 * c + 16] = every(total3, 128 * c + z, 16, 8)
+    own_v[32:48] = every(turn, 128 + x, 16, 4)
+    store_own = pltpu.make_async_copy(own_v, own3, store_sem.at[2])
+    store_own.start()
+
+    for kind, buffer in ((0, stat), (1, dstat)):
+        first_copy(buffer, kind).wait_send()
+        loop(REACH + 1, lambda d: second_copy(buffer, kind, d).wait_send())
+    g_partner.wait_send()
+    x_partner.wait_send()
+    for f in range(2):
+        pl.when(core == 0)(g_back[f].wait_send)
+        pl.when(core == 1)(g_relay[f].wait_send)
+    pl.when(core == 1)(x_ahead.wait_send)
+    for d in (1, 2, 3):
+        for i in PIECES:
+            one_x(i, d).wait_send()
+            one_y(i, d).wait_send()
+        for c, kind in ((0, 0), (0, 1), (1, 0), (1, 1), (0, 2)):
+            two(c, kind, d).wait_send()
+    for i in Z_PIECES:
+        loop(nz, lambda d: one_z(i, d).wait_send())
+    loop(nz, lambda d: three(0, d).wait_send())
+
+    store_out.wait()
+    store_grads.wait()
+    store_own.wait()
+    for c in range(2):
         loop(nz, lambda d: three(c, d).wait_recv())
-        total = every(total3, 128 * c + z, 16, 8)
-        for d in range(1, nz):
-            total = total + r3[d, pl.ds(16 * c, 16)].astype(F32)
-        low, count = HALVES[c]
-        finish(total, [(axis, low + k) for axis in "xy" for k in range(6)])
     for d in (1, 2, 3):
         two(0, 3, d).wait_recv()
-    total = every(turn, 128 + x, 16, 4)
-    for d in range(1, 4):
-        total = total + rz3[d].astype(F32)
-    finish(total, [("z", k) for k in range(Z_TAPS)])
-
-    first_copy(stat, 0).wait_send()
-    loop(REACH + 1, lambda d: second_copy(stat, 0, d).wait_send())
-    first_copy(dstat, 1).wait_send()
-    loop(REACH + 1, lambda d: second_copy(dstat, 1, d).wait_send())
-    g_partner.wait_send()
-    x_partner.wait_send()
-
-    x_or_g = ((g_back, 0), (g_relay, 1), (x_ahead, 1))
-    for copy, sender in x_or_g:
-        pl.when(core == sender)(copy.wait_send)
-    for d in range(1, 4):
-        for i in range(3):
-            one_x(i, d).wait_send()
-            one_y(i, d).wait_send()
-        for c, kind in ((0, 0), (0, 1), (1, 0), (1, 1), (0, 2), (0, 3)):
-            two(c, kind, d).wait_send()
-    loop(nz, lambda d: one_z(d).wait_send())
-    for c in range(2):
-        loop(nz, lambda d: three(c, d).wait_send())
-    store_out.wait()
-    store_grads.wait()
-
-
-def hand_over(*refs):
-    sources, targets, held, sems = refs[:3], refs[3:6], refs[6:9], refs[9]
-    into = [pltpu.make_async_copy(sources[k], held[k], sems.at[0, k]) for k in range(3)]
-    out = [pltpu.make_async_copy(held[k], targets[k], sems.at[1, k]) for k in range(3)]
-    for copy in into:
-        copy.start()
-    for k in range(3):
-        into[k].wait()
-        out[k].start()
-    for copy in out:
-        copy.wait()
+
+    for d in (1, 2, 3):
+        two(0, 3, d).wait_send()
+    loop(nz, lambda d: three(1, d).wait_send())
+
+
+def last_sum(scale, out, grads, own3, r3, rz3, *refs):
+    out_to, grads_to, wgrads, out_v, grads_v, own_v, r3_v, rz3_v, w_v, sems = refs
+
+    def copy(src, dst, k):
+        return pltpu.make_async_copy(src, dst, sems.at[k])
+
+    into = [
+        copy(own3, own_v, 0),
+        copy(r3, r3_v, 1),
+        copy(rz3, rz3_v, 2),
+        copy(out, out_v, 3),
+        copy(grads, grads_v, 4),
+    ]
+    for part in into:
+        part.start()
+    into[3].wait()
+    outward = [copy(out_v, out_to, 5)]
+    outward[0].start()
+    into[4].wait()
+    outward.append(copy(grads_v, grads_to, 6))
+    outward[1].start()
+    for part in into[:3]:
+        part.wait()
+    total = own_v[0:32]
+    for d in range(1, r3_v.shape[0]):
+        total = total + r3_v[d].astype(F32)
+    along_z = own_v[32:48]
+    for d in range(1, rz3_v.shape[0]):
+        along_z = along_z + rz3_v[d].astype(F32)
+    places = [("z", k) for k in range(16)]
+    for c, (low, count, first, length) in enumerate(HALVES):
+        taps = [(axis, low + k) for axis in "xy" for k in range(length // 8)]
+        places = places + taps + [None] * (16 - len(taps))
+    rows = jnp.concatenate([along_z, total], axis=0) * scale
+    for n in range(TAPS):
+        k = places.index(place_of(n))
+        to = 9 * (n % 3) + n // 3
+        w_v[to] = rows[k : k + 1]
+    outward.append(copy(w_v, wgrads, 7))
+    outward[2].start()
+    for part in outward:
+        part.wait()
 
 
 def local(nz, ny, scale, video_tile, clip_lengths, kernels, norm_gains, norm_shifts, cotangent):
     hbm = pl.BlockSpec(memory_space=pltpu.HBM)
-    vmem = pl.BlockSpec(memory_space=pltpu.VMEM)
     dma = pltpu.SemaphoreType.DMA
     made = pl.pallas_call(
-        functools.partial(kernel, nz, ny, scale),
+        functools.partial(kernel, nz, ny),
         out_shape=(
             jax.ShapeDtypeStruct(video_tile.shape, BF16),
             jax.ShapeDtypeStruct(video_tile.shape, BF16),
-            jax.ShapeDtypeStruct((TAPS, 1, 256), F32),
+            jax.ShapeDtypeStruct((48, 256), F32),
+            jax.ShapeDtypeStruct((nz, 32, 256), BF16),
+            jax.ShapeDtypeStruct((NX, 16, 256), BF16),
         ),
         in_specs=[hbm] * 6,
-        out_specs=(hbm, hbm, vmem),
+        out_specs=(hbm,) * 5,
         scratch_shapes=[
             pltpu.SMEM((1, 6), jnp.int32),
             pltpu.VMEM((1, 256), F32),
@@ -754,27 +792,26 @@
             pltpu.VMEM((4, 32, 256), BF16),
             pltpu.VMEM((4, 32, 256), BF16),
             pltpu.VMEM((4, 16, 256), BF16),
-            pltpu.VMEM((4, 16, 256), BF16),
             pltpu.VMEM((4, 96, 256), F32),
             pltpu.VMEM((4, 96, 256), F32),
             pltpu.VMEM((2, 128 * Z_TAPS, 128), F32),
             pltpu.VMEM((2, 256, 128), F32),
             pltpu.VMEM((8, 32, 256), BF16),
-            pltpu.VMEM((8, 32, 256), BF16),
+            pltpu.VMEM((48, 256), F32),
             pltpu.VMEM((2, 16, 16, 256), BF16),
             pltpu.VMEM((2, 16, 16, 256), BF16),
             dma((8,)),
-            dma((4,)),
-            dma((4,)),
+            dma((5,)),
+            dma((5,)),
             dma((2, REACH + 1)),
             dma((2, REACH + 1)),
-            dma((2, 3, 4)),
-            dma((2, 3, 4)),
+            dma((2, 5, 4)),
+            dma((2, 5, 4)),
             dma((4, 2, 4)),
             dma((4, 2, 4)),
-            dma((3, 8)),
-            dma((3, 8)),
-            dma((2,)),
+            dma((4, 8)),
+            dma((4, 8)),
+            dma((3,)),
         ],
         compiler_params=pltpu.CompilerParams(
             collective_id=0, has_side_effects=True, vmem_limit_bytes=60 * 1024 * 1024
@@ -782,11 +819,16 @@
         cost_estimate=pl.CostEstimate(flops=5_500_000_000, bytes_accessed=5_000_000, transcendentals=400_000),
     )(clip_lengths, norm_gains, norm_shifts, video_tile, cotangent, kernels)
     results = pl.pallas_call(
-        hand_over,
-        out_shape=tuple(jax.ShapeDtypeStruct(part.shape, part.dtype) for part in made),
-        in_specs=[hbm] * 3,
+        functools.partial(last_sum, scale),
+        out_shape=(
+            jax.ShapeDtypeStruct(video_tile.shape, BF16),
+            jax.ShapeDtypeStruct(video_tile.shape, BF16),
+            jax.ShapeDtypeStruct((TAPS, 1, 256), F32),
+        ),
+        in_specs=[hbm] * 5,
         out_specs=(hbm,) * 3,
-        scratch_shapes=[pltpu.VMEM(part.shape, part.dtype) for part in made] + [dma((2, 3))],
+        scratch_shapes=[pltpu.VMEM(part.shape, part.dtype) for part in made]
+        + [pltpu.VMEM((TAPS, 1, 256), F32), dma((8,))],
         compiler_params=pltpu.CompilerParams(vmem_limit_bytes=60 * 1024 * 1024),
     )(*made)
     return (results[0], results[1], results[2].transpose(1, 0, 2))

time: 45.1 us -> 44.4 us (0.984)
  no operation moved by 1% of the time
where the time goes in v3:
time: 44.4 us; the launch traced here: 44.3 us
  Pallas kernels  43.6 us (98%)
  between operations  0.64 us (1%)
    pallas_call x1, Pallas kernels, local(): pl.pallas_call(functools.partial(kernel, nz, ny), out_shape=(jax.ShapeDty...  41.7 us
    pallas_call x1, Pallas kernels, local(): pl.pallas_call(functools.partial(last_sum, scale), out_shape=(jax.ShapeDt...  1.92 us

profile of v3, /device:TPU:32, one launch (start us, length us, event | category | flops | bytes accessed | tf_op | source)
XLA Modules:
  0.0 44.3 jit_solution(7663441470106245019)
XLA Ops:
  0.6 41.7 %shard_map.85 = (bf16[1,2,16,16,256]{4,3,2,1,0:T(8,128)(2,1)}, bf16[1,2,16,16,256]{4,3,2,1,0:T(8,128)(2,1)}, f32[48,256]{1,0:T(8,128)}, bf16[8,32,256]{2,1,0:T(8,128)(2,1)}, bf16[4,16,256]{2,1,0:T(8,128)(2,1)}) custom-call(s32[1,6]{1,0:T(1,128)} %lens_hbm.1, f32[1,256]{1,0:T(1,128)} %gain_hbm.1, f32[1,256]{1,0:T(1,128)} %shift_hbm.1, ...), custom_call_target="tpu_custom_call" | custom-call | flops 5500000256 | bytes 5000000 | tf_op jit(solution)/shard_map/pallas_call | solution.py:754
  42.3 1.9 %shard_map.86 = (bf16[1,2,16,16,256]{4,3,2,1,0:T(8,128)(2,1)}, bf16[1,2,16,16,256]{4,3,2,1,0:T(8,128)(2,1)}, f32[27,1,256]{2,1,0:T(1,128)}) custom-call(bf16[1,2,16,16,256]{4,3,2,1,0:T(8,128)(2,1)} %get-tuple-element.11.out, bf16[1,2,16,16,256]{4,3,2,1,0:T(8,128)(2,1)} %get-tuple-element.12.grads, f32[48,256]{1,0:T(8,128)} %get-tuple-element.13.own3, ...), custom_call_target="tpu_custom_call" | custom-call | tf_op jit(solution)/shard_map/pallas_call | solution.py:821

commit v4 on v3

--- a/solution.py
+++ b/solution.py
@@ -53,14 +53,23 @@
     return jnp.where(condition, jnp.float32(1.0), jnp.float32(0.0))
 
 
-def dot(a, b, contract=(1, 0), precision=None):
+def dot(a, b, contract=(1, 0)):
     return lax.dot_general(
         a,
         b,
         (((contract[0],), (contract[1],)), ((), ())),
         preferred_element_type=F32,
-        precision=precision,
     )
+
+
+def sums_of(rows, matrix):
+    high = rows.astype(BF16)
+    rest = rows - high.astype(F32)
+    middle = rest.astype(BF16)
+    low = (rest - middle.astype(F32)).astype(BF16)
+    n = rows.shape[0]
+    parts = dot(jnp.concatenate([high, middle, low], axis=0), matrix.astype(BF16))
+    return parts[:n] + (parts[n : 2 * n] + parts[2 * n :])
 
 
 def sigmoid(z):
@@ -68,12 +77,12 @@
 
 
 def pack_rows(rows):
-    place = iota((8, 256), 0)
-    stacked = jnp.zeros((8, 256), F32)
+    place = iota((16, 256), 0)
+    stacked = jnp.zeros((16, 256), F32)
     for k, row in enumerate(rows):
         stacked = jnp.where(place == k, row, stacked)
     gather = ((iota((256, 128), 0) >> 3) == (iota((256, 128), 1) & 31)).astype(F32)
-    grouped = dot(stacked, gather, precision=lax.Precision.HIGHEST)
+    grouped = sums_of(stacked, gather)[:8]
     mine = (iota((8, 128), 1) >> 5) == iota((8, 128), 0)
     return jnp.sum(jnp.where(mine, grouped, 0.0), axis=0, keepdims=True)
 
@@ -82,7 +91,7 @@
     rows = jnp.concatenate(parts, axis=0)
     clean = jnp.where(iota(rows.shape, 1) < 32, rows, 0.0)
     matrix = (iota((128, 256), 0) == (iota((128, 256), 1) >> 3)).astype(F32)
-    wide = dot(clean, matrix, precision=lax.Precision.HIGHEST)
+    wide = sums_of(clean, matrix)
     return [wide[8 * k : 8 * k + 8] for k in range(len(parts))]
 
 
@@ -206,28 +215,32 @@
         for k, (src, dst) in enumerate(((lens_hbm, lens), (gain_hbm, gain), (shift_hbm, shift)))
     ]
     load_x.start()
+
+    barrier = pltpu.get_barrier_semaphore()
+
+    def greet(device):
+        pl.semaphore_signal(barrier, inc=1, device_id=device, device_id_type=MESH)
+
+    def greet_before(d, carry):
+        greet(at(chip_peer(chips - REACH + d)))
+        return carry
+
+    def greet_after(d, carry):
+        greet(at(chip_peer(d)))
+        return carry
+
+    greet(at(partner))
+    greet(at(beside))
+    lax.fori_loop(0, REACH, greet_before, 0)
+    far = range(REACH // NX + 1, nz - REACH // NX)
+    for d in range(1, ny):
+        greet(at(tm, y_peer(d)))
+    for d in far:
+        greet(at(z_peer(d)))
+    lax.fori_loop(1, REACH + 1, greet_after, 0)
     load_g.start()
     for copy in load_small:
         copy.start()
-
-    barrier = pltpu.get_barrier_semaphore()
-
-    def greet(device):
-        pl.semaphore_signal(barrier, inc=1, device_id=device, device_id_type=MESH)
-
-    def greet_chips(d, carry):
-        greet(at(chip_peer(d)))
-        greet(at(chip_peer(chips - d)))
-        return carry
-
-    far = range(REACH // NX + 1, nz - REACH // NX)
-    for d in far:
-        greet(at(z_peer(d)))
-    for d in range(1, ny):
-        greet(at(tm, y_peer(d)))
-    lax.fori_loop(0, REACH, lambda d, carry: greet_chips(REACH - d, carry), 0)
-    greet(at(partner))
-    greet(at(beside))
     for copy in load_k:
         copy.start()
 
@@ -301,6 +314,12 @@
     g_partner.start()
     x_partner.start()
 
+    @pl.when(core == 0)
+    def _():
+        g_back[0].start()
+        g_back[1].start()
+
+
     pixel, source = iota((256, 256), 0), iota((256, 256), 1)
     right = ((source == pixel + 1) & ((pixel & 15) != 15)).astype(BF16)
     left = ((source == pixel - 1) & ((pixel & 15) != 0)).astype(BF16)
@@ -343,11 +362,6 @@
 
     first_copy(stat, 0).wait_recv()
     loop(REACH + 1, lambda d: second_copy(stat, 0, REACH + 1 - d).start())
-
-    @pl.when(core == 0)
-    def _():
-        g_back[0].start()
-        g_back[1].start()
 
     load_k[0].wait()
     backward(0)

time: 44.4 us -> 43.7 us (0.984)
  Pallas kernels: 43.6 us -> 42.9 us
    pallas_call x1, Pallas kernels: 41.7 us -> 41 us  [local(): pl.pallas_call(functools.partial(kernel, nz, ny), out_shape=(jax.ShapeDty...]
where the time goes in v4:
time: 43.7 us; the launch traced here: 43.6 us
  Pallas kernels  42.9 us (98%)
  between operations  0.64 us (1%)
    pallas_call x1, Pallas kernels, local(): pl.pallas_call(functools.partial(kernel, nz, ny), out_shape=(jax.ShapeDty...  41 us
    pallas_call x1, Pallas kernels, local(): pl.pallas_call(functools.partial(last_sum, scale), out_shape=(jax.ShapeDt...  1.92 us

profile of v4, /device:TPU:32, one launch (start us, length us, event | category | flops | bytes accessed | tf_op | source)
XLA Modules:
  0.0 43.6 jit_solution(13376228542607230625)
XLA Ops:
  0.6 41.0 %shard_map.85 = (bf16[1,2,16,16,256]{4,3,2,1,0:T(8,128)(2,1)}, bf16[1,2,16,16,256]{4,3,2,1,0:T(8,128)(2,1)}, f32[48,256]{1,0:T(8,128)}, bf16[8,32,256]{2,1,0:T(8,128)(2,1)}, bf16[4,16,256]{2,1,0:T(8,128)(2,1)}) custom-call(s32[1,6]{1,0:T(1,128)} %lens_hbm.1, f32[1,256]{1,0:T(1,128)} %gain_hbm.1, f32[1,256]{1,0:T(1,128)} %shift_hbm.1, ...), custom_call_target="tpu_custom_call" | custom-call | flops 5500000256 | bytes 5000000 | tf_op jit(solution)/shard_map/pallas_call | solution.py:768
  41.7 1.9 %shard_map.86 = (bf16[1,2,16,16,256]{4,3,2,1,0:T(8,128)(2,1)}, bf16[1,2,16,16,256]{4,3,2,1,0:T(8,128)(2,1)}, f32[27,1,256]{2,1,0:T(1,128)}) custom-call(bf16[1,2,16,16,256]{4,3,2,1,0:T(8,128)(2,1)} %get-tuple-element.11.out, bf16[1,2,16,16,256]{4,3,2,1,0:T(8,128)(2,1)} %get-tuple-element.12.grads, f32[48,256]{1,0:T(8,128)} %get-tuple-element.13.own3, ...), custom_call_target="tpu_custom_call" | custom-call | tf_op jit(solution)/shard_map/pallas_call | solution.py:835

commit v5 on v4

--- a/solution.py
+++ b/solution.py
@@ -225,10 +225,6 @@
         greet(at(chip_peer(chips - REACH + d)))
         return carry
 
-    def greet_after(d, carry):
-        greet(at(chip_peer(d)))
-        return carry
-
     greet(at(partner))
     greet(at(beside))
     lax.fori_loop(0, REACH, greet_before, 0)
@@ -237,7 +233,6 @@
         greet(at(tm, y_peer(d)))
     for d in far:
         greet(at(z_peer(d)))
-    lax.fori_loop(1, REACH + 1, greet_after, 0)
     load_g.start()
     for copy in load_small:
         copy.start()
@@ -260,7 +255,7 @@
         sums.append(jnp.sum(values * values, axis=0, keepdims=True))
     stat[pl.ds(tm, 1)] = pack_rows(sums).reshape(1, 1, 128)
 
-    pl.semaphore_wait(barrier, 2 * REACH + len(far) + (ny - 1) + 2)
+    pl.semaphore_wait(barrier, REACH + len(far) + (ny - 1) + 2)
 
     def first_copy(buffer, kind):
         mine = buffer.at[pl.ds(tm, 1)]

time: 43.7 us -> 43.4 us (level)
  no operation moved by 1% of the time
where the time goes in v5:
time: 43.4 us; the launch traced here: 43.2 us
  Pallas kernels  42.6 us (98%)
  between operations  0.64 us (1%)
    pallas_call x1, Pallas kernels, local(): pl.pallas_call(functools.partial(kernel, nz, ny), out_shape=(jax.ShapeDty...  40.7 us
    pallas_call x1, Pallas kernels, local(): pl.pallas_call(functools.partial(last_sum, scale), out_shape=(jax.ShapeDt...  1.92 us

profile of v5, /device:TPU:32, one launch (start us, length us, event | category | flops | bytes accessed | tf_op | source)
XLA Modules:
  0.0 43.2 jit_solution(2135430373199636946)
XLA Ops:
  0.6 40.7 %shard_map.85 = (bf16[1,2,16,16,256]{4,3,2,1,0:T(8,128)(2,1)}, bf16[1,2,16,16,256]{4,3,2,1,0:T(8,128)(2,1)}, f32[48,256]{1,0:T(8,128)}, bf16[8,32,256]{2,1,0:T(8,128)(2,1)}, bf16[4,16,256]{2,1,0:T(8,128)(2,1)}) custom-call(s32[1,6]{1,0:T(1,128)} %lens_hbm.1, f32[1,256]{1,0:T(1,128)} %gain_hbm.1, f32[1,256]{1,0:T(1,128)} %shift_hbm.1, ...), custom_call_target="tpu_custom_call" | custom-call | flops 5500000256 | bytes 5000000 | tf_op jit(solution)/shard_map/pallas_call | solution.py:763
  41.3 1.9 %shard_map.86 = (bf16[1,2,16,16,256]{4,3,2,1,0:T(8,128)(2,1)}, bf16[1,2,16,16,256]{4,3,2,1,0:T(8,128)(2,1)}, f32[27,1,256]{2,1,0:T(1,128)}) custom-call(bf16[1,2,16,16,256]{4,3,2,1,0:T(8,128)(2,1)} %get-tuple-element.11.out, bf16[1,2,16,16,256]{4,3,2,1,0:T(8,128)(2,1)} %get-tuple-element.12.grads, f32[48,256]{1,0:T(8,128)} %get-tuple-element.13.own3, ...), custom_call_target="tpu_custom_call" | custom-call | tf_op jit(solution)/shard_map/pallas_call | solution.py:830

commit v6 on v5

--- a/solution.py
+++ b/solution.py
@@ -18,7 +18,7 @@
 F32 = jnp.float32
 BF16 = jnp.bfloat16
 Z_TAPS = 5
-Z_PIECES = {1: (0, 2), 4: (2, 3)}
+Z_PIECES = {0: (0, 1), 2: (1, 2), 4: (3, 2)}
 PIECES = {0: (0, 1), 2: (1, 2), 4: (3, 2), 6: (5, 3), 8: (8, 3)}
 HALVES = ((0, 8, 0, 64), (8, 3, 64, 32))
 
@@ -451,8 +451,8 @@
         return pltpu.make_async_remote_copy(
             src_ref=sz1.at[lax.rem(z + d, nz), pl.ds(low, count)],
             dst_ref=rz1.at[d, pl.ds(low, count)],
-            send_sem=three_send.at[2 + i // 4, d],
-            recv_sem=three_recv.at[2 + i // 4, d],
+            send_sem=three_send.at[2 + i // 2, d],
+            recv_sem=three_recv.at[2 + i // 2, d],
             device_id=at(z_peer(d)),
             device_id_type=MESH,
         )
@@ -482,12 +482,12 @@
                 else:
                     rows = [block[32 * q + 8 * p : 32 * q + 8 * p + 8] for q in range(4)]
                     sy1[p, slot] = jnp.concatenate(rows, axis=0).astype(BF16)
+        if step in Z_PIECES:
+            loop(nz, lambda d: one_z(step, d).start())
         if step in PIECES:
             for d in (2, 1, 3):
                 one_x(step, d).start()
                 one_y(step, d).start()
-        if step in Z_PIECES:
-            loop(nz, lambda d: one_z(step, d).start())
 
     for lag in (1, 2):
         load_k[lag].wait()
@@ -818,8 +818,8 @@
             dma((2, 5, 4)),
             dma((4, 2, 4)),
             dma((4, 2, 4)),
-            dma((4, 8)),
-            dma((4, 8)),
+            dma((5, 8)),
+            dma((5, 8)),
             dma((3,)),
         ],
         compiler_params=pltpu.CompilerParams(

time: 43.4 us -> 43.3 us (level)
  no operation moved by 1% of the time
where the time goes in v6:
time: 43.3 us; the launch traced here: 43.2 us
  Pallas kernels  42.5 us (98%)
  between operations  0.64 us (1%)
    pallas_call x1, Pallas kernels, local(): pl.pallas_call(functools.partial(kernel, nz, ny), out_shape=(jax.ShapeDty...  40.6 us
    pallas_call x1, Pallas kernels, local(): pl.pallas_call(functools.partial(last_sum, scale), out_shape=(jax.ShapeDt...  1.92 us

profile of v6, /device:TPU:32, one launch (start us, length us, event | category | flops | bytes accessed | tf_op | source)
XLA Modules:
  0.0 43.2 jit_solution(14839232653643367419)
XLA Ops:
  0.6 40.6 %shard_map.85 = (bf16[1,2,16,16,256]{4,3,2,1,0:T(8,128)(2,1)}, bf16[1,2,16,16,256]{4,3,2,1,0:T(8,128)(2,1)}, f32[48,256]{1,0:T(8,128)}, bf16[8,32,256]{2,1,0:T(8,128)(2,1)}, bf16[4,16,256]{2,1,0:T(8,128)(2,1)}) custom-call(s32[1,6]{1,0:T(1,128)} %lens_hbm.1, f32[1,256]{1,0:T(1,128)} %gain_hbm.1, f32[1,256]{1,0:T(1,128)} %shift_hbm.1, ...), custom_call_target="tpu_custom_call" | custom-call | flops 5500000256 | bytes 5000000 | tf_op jit(solution)/shard_map/pallas_call | solution.py:763
  41.2 1.9 %shard_map.86 = (bf16[1,2,16,16,256]{4,3,2,1,0:T(8,128)(2,1)}, bf16[1,2,16,16,256]{4,3,2,1,0:T(8,128)(2,1)}, f32[27,1,256]{2,1,0:T(1,128)}) custom-call(bf16[1,2,16,16,256]{4,3,2,1,0:T(8,128)(2,1)} %get-tuple-element.11.out, bf16[1,2,16,16,256]{4,3,2,1,0:T(8,128)(2,1)} %get-tuple-element.12.grads, f32[48,256]{1,0:T(8,128)} %get-tuple-element.13.own3, ...), custom_call_target="tpu_custom_call" | custom-call | tf_op jit(solution)/shard_map/pallas_call | solution.py:830

commit v7 on v6

--- a/solution.py
+++ b/solution.py
@@ -803,8 +803,8 @@
             pltpu.VMEM((4, 16, 256), BF16),
             pltpu.VMEM((4, 96, 256), F32),
             pltpu.VMEM((4, 96, 256), F32),
-            pltpu.VMEM((2, 128 * Z_TAPS, 128), F32),
-            pltpu.VMEM((2, 256, 128), F32),
+            pltpu.VMEM((2, 128 * Z_TAPS + 8, 128), F32),
+            pltpu.VMEM((2, 264, 128), F32),
             pltpu.VMEM((8, 32, 256), BF16),
             pltpu.VMEM((48, 256), F32),
             pltpu.VMEM((2, 16, 16, 256), BF16),

time: 43.3 us -> 43.3 us (level)
  no operation moved by 1% of the time
where the time goes in v7:
time: 43.3 us; the launch traced here: 43.2 us
  Pallas kernels  42.5 us (98%)
  between operations  0.64 us (1%)
    pallas_call x1, Pallas kernels, local(): pl.pallas_call(functools.partial(kernel, nz, ny), out_shape=(jax.ShapeDty...  40.6 us
    pallas_call x1, Pallas kernels, local(): pl.pallas_call(functools.partial(last_sum, scale), out_shape=(jax.ShapeDt...  1.92 us

profile of v7, /device:TPU:32, one launch (start us, length us, event | category | flops | bytes accessed | tf_op | source)
XLA Modules:
  0.0 43.2 jit_solution(17657709750935967603)
XLA Ops:
  0.6 40.6 %shard_map.85 = (bf16[1,2,16,16,256]{4,3,2,1,0:T(8,128)(2,1)}, bf16[1,2,16,16,256]{4,3,2,1,0:T(8,128)(2,1)}, f32[48,256]{1,0:T(8,128)}, bf16[8,32,256]{2,1,0:T(8,128)(2,1)}, bf16[4,16,256]{2,1,0:T(8,128)(2,1)}) custom-call(s32[1,6]{1,0:T(1,128)} %lens_hbm.1, f32[1,256]{1,0:T(1,128)} %gain_hbm.1, f32[1,256]{1,0:T(1,128)} %shift_hbm.1, ...), custom_call_target="tpu_custom_call" | custom-call | flops 5500000256 | bytes 5000000 | tf_op jit(solution)/shard_map/pallas_call | solution.py:763
  41.2 1.9 %shard_map.86 = (bf16[1,2,16,16,256]{4,3,2,1,0:T(8,128)(2,1)}, bf16[1,2,16,16,256]{4,3,2,1,0:T(8,128)(2,1)}, f32[27,1,256]{2,1,0:T(1,128)}) custom-call(bf16[1,2,16,16,256]{4,3,2,1,0:T(8,128)(2,1)} %get-tuple-element.11.out, bf16[1,2,16,16,256]{4,3,2,1,0:T(8,128)(2,1)} %get-tuple-element.12.grads, f32[48,256]{1,0:T(8,128)} %get-tuple-element.13.own3, ...), custom_call_target="tpu_custom_call" | custom-call | tf_op jit(solution)/shard_map/pallas_call | solution.py:830
